TPU v7x, 256 devices: a whole 4x4x8 slice. The times are simulated.
256 devices in a mesh: state: 8 (over z_lo, y), slab: 32 (over z_hi, x, core).
Axes of the slice: x: 4, y: 4, z: 8 (z_hi: 4, z_lo: 2; z = z_hi * 2 + z_lo), core: 2. Of those that a mesh axis runs over, the one named last changes fastest.
Arguments:
- state_images: bfloat16 [8, 2, 320, 2, 320, 128], P('state', None, 'slab'), may hold values from -6 to 6
- rot_index: int32 [8], P('state'), may hold values from 0 to 31
- counts: int32 [8], P('state'), may hold values from 16 to 64
Outputs:
- combined: float32 [2, 320, 2, 320, 128], P(None, 'slab', None, None, 'state')
All inputs are finite; a program needn't handle non-finite values.
Results may differ from a plain program's by a relative error of at most 0.022.
Values may be sent and summed in bfloat16 or wider, within the bound.
A program may use at most 192 MiB of HBM per device.

v0:
```python
import math

import jax
import jax.numpy as jnp
from jax import lax
from jax.sharding import PartitionSpec as P

ANGLES = 32


angle_step = math.pi / 120.0
count_scale = 1.0 / 64.0


def dft_tables(length):
    points = jnp.arange(length, dtype=jnp.int32)
    phases = (points[:, None] * points[None, :] % length).astype(jnp.float32) * (
        2.0 * math.pi / length
    )
    cosine = jnp.cos(phases)
    sine = jnp.sin(phases)
    forward = jnp.stack([jnp.stack([cosine, sine], 1), jnp.stack([-sine, cosine], 1)], 1)
    inverse = jnp.stack([jnp.stack([cosine, -sine], 1), jnp.stack([sine, cosine], 1)], 1) / length
    frequency = (points - length * (points >= length // 2).astype(jnp.int32)).astype(jnp.float32)
    return (forward.astype(jnp.bfloat16), inverse.astype(jnp.bfloat16), frequency)


def apply_ramp(spectrum, phases):
    real_part = spectrum[:, :, 0]
    imag_part = spectrum[:, :, 1]
    cosine = jnp.cos(phases)
    sine = jnp.sin(phases)
    return jnp.stack(
        [real_part * cosine + imag_part * sine, imag_part * cosine - real_part * sine], 2
    ).astype(jnp.bfloat16)


def shear_x(volume, shifts, tables):
    forward, inverse, frequency = tables
    length = volume.shape[3]
    spectrum = jnp.einsum("kpqn,bzqny->bzpky", forward, volume, preferred_element_type=jnp.float32)
    phases = 2.0 * math.pi / length * shifts[:, :, None, None] * frequency[None, None, :, None]
    ramped = apply_ramp(spectrum, phases)
    return jnp.einsum(
        "npqk,bzqky->bzpny", inverse, ramped, preferred_element_type=jnp.float32
    ).astype(jnp.bfloat16)


def shear_z(volume, shifts, tables):
    forward, inverse, frequency = tables
    length = volume.shape[1]
    spectrum = jnp.einsum("kpqn,bnqxy->bkpxy", forward, volume, preferred_element_type=jnp.float32)
    phases = 2.0 * math.pi / length * frequency[None, :, None, None] * shifts[:, None, :, None]
    ramped = apply_ramp(spectrum, phases)
    return jnp.einsum(
        "npqk,bkqxy->bnpxy", inverse, ramped, preferred_element_type=jnp.float32
    ).astype(jnp.bfloat16)


def body(state_images, rot_index, counts):
    slab_count = lax.axis_size("slab")
    slab_at = lax.axis_index("slab")
    coef_count = state_images.shape[1]
    z_cells = state_images.shape[2]
    x_total = state_images.shape[4]
    z_total = z_cells * slab_count
    x_cells = x_total // slab_count
    tables_x = dft_tables(x_total)
    tables_z = dft_tables(z_total)
    volume = state_images[0]
    angle_rows = jnp.repeat(rot_index, coef_count)
    count_rows = jnp.repeat(counts, coef_count)
    angle = -(angle_rows.astype(jnp.float32) - ANGLES // 2) * angle_step
    z_offsets = (slab_at * z_cells + jnp.arange(z_cells, dtype=jnp.int32)).astype(jnp.float32) - (
        z_total - 1
    ) / 2.0
    x_offsets = (slab_at * x_cells + jnp.arange(x_cells, dtype=jnp.int32)).astype(jnp.float32) - (
        x_total - 1
    ) / 2.0
    tilt_shift = -jnp.tan(angle / 2.0)[:, None] * z_offsets[None, :]
    lift_shift = jnp.sin(angle)[:, None] * x_offsets[None, :]
    first = shear_x(volume, tilt_shift, tables_x)
    columns = lax.all_to_all(first, "slab", split_axis=3, concat_axis=1, tiled=True)
    sheared = shear_z(columns, lift_shift, tables_z)
    second = lax.all_to_all(sheared, "slab", split_axis=1, concat_axis=3, tiled=True)
    third = shear_x(second, tilt_shift, tables_x)
    weights = count_rows.astype(jnp.float32) * count_scale
    weighted = third.astype(jnp.float32) * weights[:, None, None, None, None]
    return lax.psum_scatter(
        weighted.astype(jnp.bfloat16), "state", scatter_dimension=4, tiled=True
    ).astype(jnp.float32)


def solution(mesh):
    placed = (P("state", None, "slab", None, None, None), P("state"), P("state"))
    return jax.shard_map(
        body,
        mesh=mesh,
        in_specs=placed,
        out_specs=P(None, "slab", None, None, "state"),
        check_vma=False,
    )
```

profile of v0, /device:TPU:15, one launch (start us, length us, event | category | flops | bytes accessed | tf_op | source)
XLA Modules:
  0.0 349.4 jit_solution(15871803553768244478)
XLA Ops:
  6.5 0.0 copy-start
  6.5 2.6 fusion.43
  9.1 2.6 fusion.45
  11.7 3.0 fusion.39
  14.7 2.6 fusion.42
  18.1 0.2 multiply_cosine_fusion.1
  18.3 0.0 copy-start.17
  18.3 0.0 copy-start.19
  18.3 1.4 maximum_bitcast_fusion.8
  19.7 0.0 copy-start.11
  19.7 0.0 copy-start.14
  19.7 0.0 copy-done
  19.8 2.7 fusion.17
  22.5 0.0 copy-start.4
  22.6 2.1 add_convert_fusion.2
  24.7 0.1 maximum_bitcast_fusion.6
  24.9 0.0 copy-start.8
  24.9 1.0 copy-done.5
  25.8 0.3 copy-done.8
  26.1 3.0 fusion.1
  29.2 5.0 %copy.34 = bf16[2,10,2,320,128]{4,2,1,0,3:T(2,128)(2,1)} copy(bf16[2,10,2,320,128]{4,3,2,1,0:T(8,128)(2,1)S(1)} %fusion.1) | data formatting | bytes 6553600 | tf_op jit(solution)/shard_map/convert_element_type | solution.py:46
  34.2 11.9 %all-to-all-start = ((bf16[2,10,2,320,128]{4,2,1,0,3:T(2,128)(2,1)}), bf16[2,10,2,320,128]{4,2,1,0,3:T(2,128)(2,1)S(1)}, u32[]{:S(2)}, u32[]{:S(2)}) async-start(bf16[2,10,2,320,128]{4,2,1,0,3:T(2,128)(2,1)} %copy.34), calls=%async_computation | async-start | bytes 6553600 | tf_op jit(solution)/shard_map/all_to_all | solution.py:83
  46.1 0.2 multiply_cosine_fusion
  46.3 70.7 %all-to-all-done = bf16[2,10,2,320,128]{4,2,1,0,3:T(2,128)(2,1)S(1)} async-done(((bf16[2,10,2,320,128]{4,2,1,0,3:T(2,128)(2,1)}), bf16[2,10,2,320,128]{4,2,1,0,3:T(2,128)(2,1)S(1)}, u32[]{:S(2)}, u32[]{:S(2)}) %all-to-all-start) | async-done | bytes 3276832 | tf_op jit(solution)/shard_map/all_to_all | solution.py:83
  117.0 2.2 copy.36
  119.3 2.7 fusion.20
  122.0 0.0 copy-start.9
  122.0 2.1 add_convert_fusion.1
  124.2 0.0 copy-done.6
  124.2 0.0 copy-done.9
  124.2 3.0 fusion.2
  127.2 5.0 %copy.38 = bf16[2,320,2,10,128]{4,2,3,0,1:T(2,128)(2,1)} copy(bf16[2,320,2,10,128]{4,1,2,3,0:T(8,128)(2,1)S(1)} %fusion.2) | data formatting | bytes 6553600 | tf_op jit(solution)/shard_map/convert_element_type | solution.py:57
  132.2 11.1 %all-to-all-start.1 = ((bf16[2,320,2,10,128]{4,2,3,0,1:T(2,128)(2,1)}), bf16[2,320,2,10,128]{4,2,3,0,1:T(2,128)(2,1)S(1)}, u32[]{:S(2)}, u32[]{:S(2)}) async-start(bf16[2,320,2,10,128]{4,2,3,0,1:T(2,128)(2,1)} %copy.38), calls=%async_computation.1 | async-start | bytes 6553600 | tf_op jit(solution)/shard_map/all_to_all | solution.py:85
  143.3 0.3 all-reduce.3.cloned.1.call-start
  144.2 75.0 %all-to-all-done.1 = bf16[2,320,2,10,128]{4,2,3,0,1:T(2,128)(2,1)S(1)} async-done(((bf16[2,320,2,10,128]{4,2,3,0,1:T(2,128)(2,1)}), bf16[2,320,2,10,128]{4,2,3,0,1:T(2,128)(2,1)S(1)}, u32[]{:S(2)}, u32[]{:S(2)}) %all-to-all-start.1) | async-done | bytes 3276832 | tf_op jit(solution)/shard_map/all_to_all | solution.py:85
  219.3 3.2 copy.40
  222.5 2.8 fusion.23
  225.3 0.0 copy-start.10
  225.4 2.1 add_convert_fusion
  227.5 3.0 fusion
  230.5 7.8 %copy.44 = bf16[2,10,2,320,128]{3,2,1,0,4:T(2,128)(2,1)} copy(bf16[2,10,2,320,128]{4,3,2,1,0:T(8,128)(2,1)S(1)} %fusion) | data formatting | bytes 6553600 | tf_op jit(solution)/shard_map/convert_element_type | solution.py:90
  238.3 0.0 all-reduce.3.cloned.1.call-update
  238.3 0.6 copy-done.21
  239.0 0.6 dynamic-slice
  240.2 99.8 %all-reduce.3.cloned.1.call-done = bf16[2,10,2,320,128]{3,2,1,0,4:T(2,128)(2,1)} async-done(((bf16[2,10,2,320,128]{3,2,1,0,4:T(2,128)(2,1)}), bf16[2,10,2,320,128]{3,2,1,0,4:T(2,128)(2,1)}) %all-reduce.3.cloned.1.call-update) | async-done | bytes 3276816
  340.0 1.4 dynamic-slice_convert_fusion
  341.4 1.1 copy.45
  342.5 0.0 copy-done.1
  (31 shorter events, 0.1 us)
Async XLA Ops:
  6.5 13.2 %copy-start = (bf16[1,2,10,2,320,128]{5,4,3,2,1,0:T(8,128)(2,1)S(1)}, bf16[1,2,10,2,320,128]{5,4,3,2,1,0:T(8,128)(2,1)}, u32[]{:S(2)}) copy-start(bf16[1,2,10,2,320,128]{5,4,3,2,1,0:T(8,128)(2,1)} %param.3) | copy-start | bytes 9830404
  18.3 4.2 %copy-start.17 = (f32[2,10,320]{2,1,0:T(8,128)}, f32[2,10,320]{2,1,0:T(8,128)S(1)}, u32[]{:S(2)}) copy-start(f32[2,10,320]{2,1,0:T(8,128)S(1)} %get-tuple-element.17) | copy-start | bytes 76804
  18.3 4.2 %copy-start.19 = (f32[2,10,320]{2,1,0:T(8,128)}, f32[2,10,320]{2,1,0:T(8,128)S(1)}, u32[]{:S(2)}) copy-start(f32[2,10,320]{2,1,0:T(8,128)S(1)} %get-tuple-element.18) | copy-start | bytes 76804
  19.7 2.8 copy-start.11
  19.7 2.8 copy-start.14
  22.5 2.2 copy-start.2
  22.5 2.2 copy-start.3
  22.5 2.2 copy-start.4
  24.9 1.0 copy-start.5
  24.9 1.3 copy-start.8
  34.2 82.8 %all-to-all-start = ((bf16[2,10,2,320,128]{4,2,1,0,3:T(2,128)(2,1)}), bf16[2,10,2,320,128]{4,2,1,0,3:T(2,128)(2,1)S(1)}, u32[]{:S(2)}, u32[]{:S(2)}) async-start(bf16[2,10,2,320,128]{4,2,1,0,3:T(2,128)(2,1)} %copy.34), calls=%async_computation | async-start | bytes 6553600 | tf_op jit(solution)/shard_map/all_to_all | solution.py:83
  117.0 2.3 copy-start.12
  117.0 2.3 copy-start.15
  122.0 2.2 copy-start.6
  122.0 2.2 copy-start.9
  132.2 87.0 %all-to-all-start.1 = ((bf16[2,320,2,10,128]{4,2,3,0,1:T(2,128)(2,1)}), bf16[2,320,2,10,128]{4,2,3,0,1:T(2,128)(2,1)S(1)}, u32[]{:S(2)}, u32[]{:S(2)}) async-start(bf16[2,320,2,10,128]{4,2,3,0,1:T(2,128)(2,1)} %copy.38), calls=%async_computation.1 | async-start | bytes 6553600 | tf_op jit(solution)/shard_map/all_to_all | solution.py:85
  143.3 196.7 %all-reduce.3.cloned.1.call-start = ((), (), s32[]{:S(2)}) async-start(), calls=%async_computation.2 | async-start | bytes 7864320
  219.3 3.2 copy-start.13
  219.3 3.2 copy-start.16
  222.5 2.8 copy-start.18
  222.5 2.8 copy-start.20
  225.3 2.2 copy-start.7
  225.3 2.2 copy-start.10
  238.3 0.7 copy-start.21
  238.3 104.2 %copy-start.1 = (bf16[1,2,10,2,320,128]{5,4,3,2,1,0:T(8,128)(2,1)S(1)}, bf16[1,2,10,2,320,128]{5,4,3,2,1,0:T(8,128)(2,1)}, u32[]{:S(2)}) copy-start(bf16[1,2,10,2,320,128]{5,4,3,2,1,0:T(8,128)(2,1)} %param.3) | copy-start | bytes 9830404
Sparse Core Ops, SparseCore 0:
  238.5 101.5 all-reduce.2
where the time goes:
time: 353 us; the launch traced here: 349 us
  waiting for transfers between devices  246 us (70%)
  local copies, waits for them, and re-layouts  27 us (8%)
  starting transfers between devices  23.2 us (7%)
  other arithmetic  20.4 us (6%)
  matrix products  17.3 us (5%)
  between operations  15.9 us (5%)
    unnamed x2, waiting for transfers between devices  99.8 us
    all_to_all x1, waiting for transfers between devices, body(): lax.all_to_all(sheared, 'slab', split_axis=1, concat_axis=3, tiled=True)  75 us
    all_to_all x1, waiting for transfers between devices, body(): lax.all_to_all(first, 'slab', split_axis=3, concat_axis=1, tiled=True)  70.7 us
    all_to_all x1, starting transfers between devices, body(): lax.all_to_all(first, 'slab', split_axis=3, concat_axis=1, tiled=True)  11.9 us
    another operation x5, other arithmetic  11.6 us
    all_to_all x1, starting transfers between devices, body(): lax.all_to_all(sheared, 'slab', split_axis=1, concat_axis=3, tiled=True)  11.1 us
    convert_element_type x1, local copies, waits for them, and re-layouts, body(): weighted.astype(jnp.bfloat16)  7.8 us
  transfers between devices with their start and end apart: 3, of which 3 were waited for; matrix products, arithmetic and copies ran while one was open for 0% of the time, Pallas kernels for 0%

commit v1 on v0

v1 whole, which is shorter than its diff:
```python
import math

import jax
import jax.numpy as jnp
import numpy as np
from jax import lax
from jax.experimental import pallas as pl
from jax.experimental.pallas import tpu as pltpu
from jax.sharding import PartitionSpec as P

N = 320
HALF = N // 2
ANGLES = 32
LANES = 640
PAD = 384
WIDE = 2 * PAD
BLOCK = 80
CHUNKS = 4
PACKED = 112
MESH = pl.DeviceIdType.MESH
f32 = jnp.float32
bf16 = jnp.bfloat16


def packed_lane(part, x):
    return np.where(x < 256, part * 256 + x, 512 + part * 64 + (x - 256))


def host_tables():
    points = np.arange(N)
    phase = (points[:, None] * points[None, :] % N) * (2.0 * math.pi / N)
    cosine = np.cos(phase)
    sine = np.sin(phase)
    forward = np.zeros((2, N, 2, PAD))
    forward[0, :, 0, :N] = cosine
    forward[1, :, 0, :N] = sine
    forward[0, :, 1, :N] = -sine
    forward[1, :, 1, :N] = cosine
    forward = forward.reshape(2 * N, WIDE)
    inverse = np.zeros((2, PAD, 2, N))
    inverse[0, :N, 0] = cosine / N
    inverse[1, :N, 0] = -sine / N
    inverse[0, :N, 1] = sine / N
    inverse[1, :N, 1] = cosine / N
    inverse = inverse.reshape(WIDE, 2 * N)
    order = np.zeros(2 * N, np.int64)
    for part in range(2):
        order[packed_lane(part, points)] = part * N + points
    angle = -(np.arange(ANGLES) - ANGLES // 2) * math.pi / 120.0
    shifts = np.stack([-np.tan(angle / 2.0), np.sin(angle)])
    return (
        jnp.asarray(forward.astype(jnp.bfloat16)),
        jnp.asarray(inverse[:, order].astype(jnp.bfloat16)),
        jnp.asarray(forward[order].astype(jnp.bfloat16)),
        jnp.asarray(np.concatenate([cosine, sine]).astype(jnp.bfloat16)),
        jnp.asarray((np.concatenate([cosine, sine]) / N).astype(jnp.bfloat16)),
        jnp.asarray(shifts.astype(np.float32)),
    )


def turn(turns):
    half = (turns - jnp.floor(turns + 0.5)) * math.pi
    sq = half * half
    s = -1.0 / 39916800.0
    for c in (1.0 / 362880.0, -1.0 / 5040.0, 1.0 / 120.0, -1.0 / 6.0, 1.0):
        s = s * sq + c
    s = s * half
    c = 1.0 / 479001600.0
    for k in (-1.0 / 3628800.0, 1.0 / 40320.0, -1.0 / 720.0, 1.0 / 24.0, -0.5, 1.0):
        c = c * sq + k
    return 1.0 - 2.0 * s * s, 2.0 * s * c


def centred(index):
    return jnp.where(index >= HALF, index - N, index).astype(f32)


def kernel(
    rot, counts, shifts, image, fwd_hbm, inv_hbm, fwd3_hbm, fz_hbm, gz_hbm,
    out,
    v, fwd, inv, fwd3, fz, gz,
    cos_x, sin_x, cos_z, sin_z,
    xsend, xrecv, zsend, planes, rsend, rrecv, fsend, frecv,
    turned, second, total, packed, final,
    load_sem, local_sem, xs_sem, xr_sem, zs_sem, zr_sem, ys_sem, yr_sem, fs_sem, fr_sem,
):
    state = lax.axis_index("state")
    slab = lax.axis_index("slab")
    zlo = state // 4
    y = state % 4
    zhi = slab // 8
    x = (slab % 8) // 2
    core = slab % 2
    me = slab % 8

    loads = []
    for i, (src, dst) in enumerate(
        ((image, v), (fwd_hbm, fwd), (inv_hbm, inv), (fz_hbm, fz), (gz_hbm, gz), (fwd3_hbm, fwd3))
    ):
        copy = pltpu.make_async_copy(src, dst, load_sem.at[i])
        copy.start()
        loads.append(copy)

    barrier = pltpu.get_barrier_semaphore()

    def greet(i, _):
        at = lax.rem(zlo * 32 + slab + i, 64)
        pl.semaphore_signal(
            barrier, inc=1,
            device_id={"state": (at // 32) * 4 + y, "slab": lax.rem(at, 32)},
            device_id_type=MESH,
        )
        return 0

    lax.fori_loop(1, 64, greet, 0)
    for i in range(1, 4):
        pl.semaphore_signal(
            barrier, inc=1,
            device_id={"state": zlo * 4 + lax.rem(y + i, 4), "slab": slab},
            device_id_type=MESH,
        )

    tilt = shifts[0, rot[0]]
    lift = shifts[1, rot[0]]
    weight = counts[0].astype(f32) * (1.0 / 64.0)
    centre = (N - 1) / 2.0

    for copy in loads[:3]:
        copy.wait()

    row_freq = centred(lax.broadcasted_iota(jnp.int32, (8, PAD), 1)) * (1.0 / N)

    def first(pair, _):
        blocks = [v[coef, 2 * pair + i] for coef in range(2) for i in range(2)]
        left = jnp.concatenate(blocks, axis=1)
        spectrum = lax.dot_general(left, fwd[...], (((0,), (0,)), ((), ())), preferred_element_type=f32)
        ramped = []
        for b in range(4):
            shift = tilt * ((slab * 10 + 2 * pair + b % 2).astype(f32) - centre)
            cosine, sine = turn(row_freq * shift)
            cosine = jnp.broadcast_to(cosine[0:1], (128, PAD))
            sine = jnp.broadcast_to(sine[0:1], (128, PAD))
            re = spectrum[128 * b : 128 * (b + 1), :PAD]
            im = spectrum[128 * b : 128 * (b + 1), PAD:]
            ramped.append(
                jnp.concatenate([re * cosine + im * sine, im * cosine - re * sine], axis=1).astype(bf16)
            )
        moved = jnp.dot(jnp.concatenate(ramped, axis=0), inv[...], preferred_element_type=f32)
        at = pl.ds(pl.multiple_of(pair * 16, 16), 16)
        for coef in range(2):
            for low in range(2):
                for yy in range(4):
                    for h in range(2):
                        q = low * 64 + yy * 16 + h * 8
                        piece = jnp.concatenate(
                            [moved[256 * coef + q : 256 * coef + q + 8],
                             moved[256 * coef + 128 + q : 256 * coef + 128 + q + 8]], axis=0)
                        xsend[(low * 2 + h) * 2 + coef, yy, at, :] = piece.astype(bf16)
        return 0

    lax.fori_loop(0, 5, first, 0)

    pl.semaphore_wait(barrier, 66)

    def chunk_y(t):
        return lax.rem(y + 1 + t, 4)

    def x_copies(t):
        yy = chunk_y(t)
        out_copies = []
        for o in range(1, 8):
            gx = lax.rem(x + o // 2, 4)
            gc = lax.rem(core + o, 2)
            out_copies.append(pltpu.make_async_remote_copy(
                src_ref=xsend.at[gx * 2 + gc, yy], dst_ref=xrecv.at[t, me],
                send_sem=xs_sem.at[t, o - 1], recv_sem=xr_sem.at[t, o - 1],
                device_id={"slab": zhi * 8 + gx * 2 + gc}, device_id_type=MESH))
        own = pltpu.make_async_copy(xsend.at[me, yy], xrecv.at[t, me], local_sem.at[t])
        return out_copies, own

    def z_copies(t):
        out_copies = []
        for o in range(1, 4):
            gz_at = lax.rem(zhi + o, 4)
            out_copies.append(pltpu.make_async_remote_copy(
                src_ref=zsend.at[t, gz_at],
                dst_ref=planes.at[t, :, pl.ds(pl.multiple_of(zhi * BLOCK, 16), BLOCK), :],
                send_sem=zs_sem.at[t, o - 1], recv_sem=zr_sem.at[t, o - 1],
                device_id={"slab": gz_at * 8 + me}, device_id_type=MESH))
        own = pltpu.make_async_copy(
            zsend.at[t, zhi], planes.at[t, :, pl.ds(pl.multiple_of(zhi * BLOCK, 16), BLOCK), :],
            local_sem.at[CHUNKS + t])
        return out_copies, own

    def y_copy(t):
        return pltpu.make_async_remote_copy(
            src_ref=rsend.at[t], dst_ref=rrecv.at[t],
            send_sem=ys_sem.at[t], recv_sem=yr_sem.at[t],
            device_id={"state": zlo * 4 + chunk_y(t)}, device_id_type=MESH)

    def start(copies):
        remote, own = copies
        for copy in remote:
            copy.start()
        own.start()

    def arrive(copies):
        remote, own = copies
        own.wait()
        for copy in remote:
            copy.wait_recv()

    xc = [x_copies(t) for t in range(CHUNKS)]
    zc = [z_copies(t) for t in range(CHUNKS)]
    yc = [y_copy(t) for t in range(CHUNKS - 1)]
    start(xc[0])

    def tables(i, _):
        rows = pl.ds(pl.multiple_of(i * 16, 16), 16)
        row = lax.broadcasted_iota(jnp.int32, (16, PAD), 0) + i * 16
        lane = lax.broadcasted_iota(jnp.int32, (16, PAD), 1)
        cosine, sine = turn(centred(lane) * (tilt * (row.astype(f32) - centre)) * (1.0 / N))
        cos_x[rows, :] = cosine
        sin_x[rows, :] = sine
        at = jnp.where(lane >= N, lane - 64, lane)
        cosine, sine = turn(centred(row) * (lift * (at.astype(f32) - centre)) * (1.0 / N))
        cos_z[rows, :] = cosine
        sin_z[rows, :] = sine
        return 0

    lax.fori_loop(0, N // 16, tables, 0)
    for copy in loads[3:]:
        copy.wait()

    def transpose(t):
        for lane in range(5):
            for g in range(8):
                turned[lane, BLOCK * g : BLOCK * (g + 1), :] = xrecv[
                    t, g, :, 128 * lane : 128 * (lane + 1)].astype(f32)
        for lane in range(5):
            for m in range(8):
                zsend[t, m // 2, m % 2, :, 128 * lane : 128 * (lane + 1)] = turned[
                    lane, pl.ds(m, BLOCK, stride=8), :].astype(bf16)

    lane128 = lax.broadcasted_iota(jnp.int32, (N, 128), 1)

    def swap(left, right, paired):
        if paired:
            return right, -left
        l = pltpu.roll(left, 64, 1)
        r = pltpu.roll(right, 64, 1)
        return jnp.where(lane128 < 64, l, -l), jnp.where(lane128 < 64, r, -r)

    def shear_planes(t):
        units = [((e, j), (e, 2 + j), j) for e in range(2) for j in range(2)] + [((0, 4), (1, 4), 2)]
        for (ea, ta), (eb, tb), tile in units:
            data = jnp.concatenate(
                [planes[t, ea, :, 128 * ta : 128 * (ta + 1)], planes[t, eb, :, 128 * tb : 128 * (tb + 1)]], axis=1)
            both = jnp.dot(fz[...], data, preferred_element_type=f32)
            cosine = cos_z[:, 128 * tile : 128 * (tile + 1)]
            sine = sin_z[:, 128 * tile : 128 * (tile + 1)]
            near, far = [], []
            for s in range(2):
                tc = both[:N, 128 * s : 128 * (s + 1)]
                ts = both[N:, 128 * s : 128 * (s + 1)]
                near.append(cosine * tc - sine * ts)
                far.append(cosine * ts + sine * tc)
            far = swap(far[0], far[1], tile < 2)
            ramped = jnp.concatenate([near[0] + far[0], near[1] + far[1]], axis=1).astype(bf16)
            both = jnp.dot(gz[...], ramped, preferred_element_type=f32)
            far = swap(both[N:, :128], both[N:, 128:], tile < 2)
            second[ea, :, 128 * ta : 128 * (ta + 1)] = (both[:N, :128] - far[0]).astype(bf16)
            second[eb, :, 128 * tb : 128 * (tb + 1)] = (both[:N, 128:] - far[1]).astype(bf16)
        for e in range(2):
            spectrum = jnp.dot(second[e], fwd3[...], preferred_element_type=f32)
            re, im = spectrum[:, :PAD], spectrum[:, PAD:]
            cosine, sine = cos_x[...], sin_x[...]
            ramped = jnp.concatenate([re * cosine + im * sine, im * cosine - re * sine], axis=1).astype(bf16)
            rsend[t, e] = (jnp.dot(ramped, inv[...], preferred_element_type=f32) * weight).astype(bf16)

    for t in range(CHUNKS):
        arrive(xc[t])
        if t + 1 < CHUNKS:
            start(xc[t + 1])
        transpose(t)
        start(zc[t])
        if t >= 1:
            arrive(zc[t - 1])
            shear_planes(t - 1)
            yc[t - 1].start()
    arrive(zc[CHUNKS - 1])
    shear_planes(CHUNKS - 1)
    for copy in yc:
        copy.wait_recv()

    def add(i, _):
        rows = pl.ds(pl.multiple_of(i * 16, 16), 16)
        for e in range(2):
            acc = rsend[CHUNKS - 1, e, rows, :].astype(f32)
            for t in range(CHUNKS - 1):
                acc = acc + rrecv[t, e, rows, :].astype(f32)
            total[e, rows, :] = acc
        return 0

    lax.fori_loop(0, N // 16, add, 0)

    target = (x // 2) * 4 + y
    slot = ((zlo * 2 + x % 2) * 4 + zhi) * 2 + core

    packed[100:PACKED, :] = jnp.zeros((PACKED - 100, 128), f32)

    def pack(q, _):
        for i in range(4):
            for e in range(2):
                for b in range(5):
                    rows = total[e, pl.ds(pl.multiple_of(q * 40, 8), 40), 128 * b : 128 * (b + 1)]
                    at = (e * 5 + b) * 10
                    packed[at : at + 10, :] = rows[10 * i : 10 * i + 10]
            fsend[q * 4 + i] = packed[...].astype(bf16)
        return 0

    lax.fori_loop(0, 8, pack, 0)

    def f_copy(o):
        to = lax.rem(slab + o, 32)
        return pltpu.make_async_remote_copy(
            src_ref=fsend.at[to], dst_ref=frecv.at[slot],
            send_sem=fs_sem.at[o], recv_sem=fr_sem.at[slot],
            device_id={"state": target, "slab": to}, device_id_type=MESH)

    def f_own():
        return pltpu.make_async_copy(fsend.at[slab], frecv.at[slot], fr_sem.at[slot])

    for o in range(1, 32):
        f_copy(o).start()

    @pl.when(target == state)
    def _():
        f_own().start()

    @pl.when(target != state)
    def _():
        f_copy(0).start()

    for t in range(CHUNKS):
        for copy in xc[t][0] + zc[t][0]:
            copy.wait_send()
    for copy in yc:
        copy.wait_send()

    def land(i, _):
        pltpu.make_async_copy(fsend.at[0], frecv.at[i], fr_sem.at[i]).wait()
        return 0

    lax.fori_loop(0, 32, land, 0)

    for h in range(2):
        for zz in range(4):
            for coef in range(2):
                at = (h * 4 + zz) * 2 + coef
                packed[...] = frecv[at].astype(f32) + frecv[16 + at].astype(f32)
                for e in range(2):
                    row = 8 * h + 2 * zz + e
                    for b in range(5):
                        piece = packed[(e * 5 + b) * 10 : (e * 5 + b) * 10 + 10, :]
                        base = coef * N + row
                        if b < 4:
                            final[b % 2, pl.ds(base + 16 * (b // 2), 10, stride=32), :] = piece
                        else:
                            final[2, pl.ds(base, 10, stride=32), :] = piece
                            final[2, pl.ds(base + 16, 10, stride=32), :] = pltpu.roll(piece, 64, 1)
    out[:, 0:128] = final[0]
    out[:, 128:256] = final[1]
    out[:, 256:320] = final[2][:, :64]

    for o in range(1, 32):
        f_copy(o).wait_send()

    @pl.when(target != state)
    def _():
        f_copy(0).wait_send()


def body(state_images, rot_index, counts):
    fwd, inv, fwd3, fz, gz, shifts = host_tables()
    image = state_images.reshape(2, 10, 2 * N, 128)
    smem = pl.BlockSpec(memory_space=pltpu.SMEM)
    anywhere = pl.BlockSpec(memory_space=pl.ANY)
    dma = pltpu.SemaphoreType.DMA
    vmem = pltpu.VMEM
    out = pl.pallas_call(
        kernel,
        name="shears",
        out_shape=jax.ShapeDtypeStruct((640, N), f32),
        in_specs=[smem, smem, smem] + [anywhere] * 6,
        out_specs=pl.BlockSpec(memory_space=vmem),
        scratch_shapes=[
            vmem(image.shape, bf16), vmem(fwd.shape, bf16), vmem(inv.shape, bf16),
            vmem(fwd3.shape, bf16), vmem(fz.shape, bf16), vmem(gz.shape, bf16),
            vmem((N, PAD), f32), vmem((N, PAD), f32), vmem((N, PAD), f32), vmem((N, PAD), f32),
            vmem((8, 4, BLOCK, LANES), bf16),
            vmem((CHUNKS, 8, BLOCK, LANES), bf16),
            vmem((CHUNKS, 4, 2, BLOCK, LANES), bf16),
            vmem((CHUNKS, 2, N, LANES), bf16),
            vmem((CHUNKS, 2, N, LANES), bf16),
            vmem((CHUNKS - 1, 2, N, LANES), bf16),
            vmem((32, PACKED, 128), bf16),
            vmem((32, PACKED, 128), bf16),
            vmem((5, 640, 128), f32),
            vmem((2, N, LANES), bf16),
            vmem((2, N, LANES), f32),
            vmem((PACKED, 128), f32),
            vmem((3, 640, 128), f32),
            dma((6,)), dma((2 * CHUNKS,)),
            dma((CHUNKS, 7)), dma((CHUNKS, 7)),
            dma((CHUNKS, 3)), dma((CHUNKS, 3)),
            dma((CHUNKS - 1,)), dma((CHUNKS - 1,)),
            dma((32,)), dma((32,)),
        ],
        compiler_params=pltpu.CompilerParams(
            collective_id=0, has_side_effects=True, vmem_limit_bytes=60 * 1024 * 1024),
        cost_estimate=pl.CostEstimate(flops=13_000_000_000, bytes_accessed=8_000_000, transcendentals=0),
    )(rot_index, counts, shifts, image, fwd, inv, fwd3, fz, gz)
    return out.reshape(2, 10, 2, 16, N).swapaxes(3, 4)


def solution(mesh):
    placed = (P("state", None, "slab", None, None, None), P("state"), P("state"))
    return jax.shard_map(
        body,
        mesh=mesh,
        in_specs=placed,
        out_specs=P(None, "slab", None, None, "state"),
        check_vma=False,
    )
```

time: 353 us -> 161 us (0.46); the launches traced: 349 us -> 161 us
  waiting for transfers between devices: 246 us -> 0 us
  Pallas kernels: 0 us -> 158 us
  local copies, waits for them, and re-layouts: 27 us -> 2.22 us
  starting transfers between devices: 23.2 us -> 0 us
  other arithmetic: 20.4 us -> 0 us
  matrix products: 17.3 us -> 0 us
  between operations: 15.9 us -> 1.31 us
    pallas_call x0 -> x1, Pallas kernels: none -> 158 us  [body(): pl.pallas_call(kernel, name='shears', out_shape=jax.ShapeDtypeStruct((640...]
    all_to_all x2 -> x0, waiting for transfers between devices: 146 us -> none  [the longest x1 75 us: body(): lax.all_to_all(sheared, 'slab', split_axis=1, concat_axis=3, tiled=True)]
    unnamed x2 -> x0, waiting for transfers between devices: 99.8 us -> none
    all_to_all x2 -> x0, starting transfers between devices: 22.9 us -> none  [the longest x1 11.9 us: body(): lax.all_to_all(first, 'slab', split_axis=3, concat_axis=1, tiled=True)]
    convert_element_type x4 -> x0, local copies, waits for them, and re-layouts: 19 us -> none  [the longest x1 7.8 us: body(): weighted.astype(jnp.bfloat16)]
    dot_general x6 -> x0, matrix products: 17.3 us -> none  [the longest x2 6.01 us: shear_x(): jnp.einsum('npqk,bzqky->bzpny', inverse, ramped, preferred_element_type=j...]
    another operation x7 -> x0, other arithmetic: 13.1 us -> none
    all_to_all x2 -> x0, local copies, waits for them, and re-layouts: 5.44 us -> none  [the longest x1 3.19 us: body(): lax.all_to_all(sheared, 'slab', split_axis=1, concat_axis=3, tiled=True)]
  transfers between devices with their start and end apart: 3 -> 0, of which waited for: 3 -> 0; matrix products, arithmetic and copies ran while one was open for 0% -> 0% of each run, Pallas kernels for 0% -> 0%
where the time goes in v1:
time: 161 us
  Pallas kernels  158 us (98%)
  local copies, waits for them, and re-layouts  2.22 us (1%)
    pallas_call x1, Pallas kernels, body(): pl.pallas_call(kernel, name='shears', out_shape=jax.ShapeDtypeStruct((640...  158 us

profile of v1, /device:TPU:15, one launch (start us, length us, event | category | flops | bytes accessed | tf_op | source)
XLA Modules:
  0.0 161.3 jit_solution(3772496012716842470)
XLA Ops:
  1.3 157.8 %shears.1 = f32[640,320]{1,0:T(8,128)} custom-call(s32[1]{0:T(128)S(6)} %copy.11.rot, s32[1]{0:T(128)S(6)} %copy.12.counts, f32[2,32]{1,0:T(2,128)} %constant.17.clone.shifts, bf16[2,10,640,128]{3,2,1,0:T(8,128)(2,1)} %bitcast.5, bf16[640,768]{1,0:T(8,128)(2,1)} %constant.12.clone.fwd_hbm, bf16[768,640]{1,0:T(8,128)(2,1)} %constant.13.clone.inv_hbm, ...), custom_call_target="tpu_custom_call" | custom-call | flops 12999999488 | bytes 8000000 | tf_op jit(solution)/shard_map/shears/pallas_call | solution.py:391
  159.1 2.2 %copy.13 = f32[2,10,2,320,16]{3,4,2,1,0:T(8,128)} copy(f32[2,10,2,320,16]{3,4,2,1,0:T(8,128)} %bitcast.4) | data formatting | bytes 1638400

commit v2 on v1

--- a/solution.py
+++ b/solution.py
@@ -16,14 +16,16 @@
 WIDE = 2 * PAD
 BLOCK = 80
 CHUNKS = 4
-PACKED = 112
+PACKED = 64
+FILLED = 50
+RING = 8
 MESH = pl.DeviceIdType.MESH
 f32 = jnp.float32
 bf16 = jnp.bfloat16
 
 
 def packed_lane(part, x):
-    return np.where(x < 256, part * 256 + x, 512 + part * 64 + (x - 256))
+    return np.where(x < 256, x // 128 * 256 + part * 128 + x % 128, 512 + part * 64 + (x - 256))
 
 
 def host_tables():
@@ -81,8 +83,8 @@
     v, fwd, inv, fwd3, fz, gz,
     cos_x, sin_x, cos_z, sin_z,
     xsend, xrecv, zsend, planes, rsend, rrecv, fsend, frecv,
-    turned, second, total, packed, final,
-    load_sem, local_sem, xs_sem, xr_sem, zs_sem, zr_sem, ys_sem, yr_sem, fs_sem, fr_sem,
+    params, turned, second, total, packed, final,
+    load_sem, local_sem, ps_sem, pr_sem, xs_sem, xr_sem, zs_sem, zr_sem, ys_sem, yr_sem, fs_sem, fr_sem,
 ):
     state = lax.axis_index("state")
     slab = lax.axis_index("slab")
@@ -92,6 +94,7 @@
     x = (slab % 8) // 2
     core = slab % 2
     me = slab % 8
+    spot = zhi * 2 + zlo
 
     loads = []
     for i, (src, dst) in enumerate(
@@ -155,7 +158,7 @@
                         piece = jnp.concatenate(
                             [moved[256 * coef + q : 256 * coef + q + 8],
                              moved[256 * coef + 128 + q : 256 * coef + 128 + q + 8]], axis=0)
-                        xsend[(low * 2 + h) * 2 + coef, yy, at, :] = piece.astype(bf16)
+                        xsend[(coef * 2 + h) * 2 + low, yy, at, :] = piece.astype(bf16)
         return 0
 
     lax.fori_loop(0, 5, first, 0)
@@ -180,16 +183,14 @@
 
     def z_copies(t):
         out_copies = []
-        for o in range(1, 4):
-            gz_at = lax.rem(zhi + o, 4)
+        dst = planes.at[t, zlo, pl.ds(pl.multiple_of(zhi * BLOCK, 16), BLOCK), :]
+        for o in range(1, RING):
+            to = lax.rem(spot + o, RING)
             out_copies.append(pltpu.make_async_remote_copy(
-                src_ref=zsend.at[t, gz_at],
-                dst_ref=planes.at[t, :, pl.ds(pl.multiple_of(zhi * BLOCK, 16), BLOCK), :],
+                src_ref=zsend.at[t, to], dst_ref=dst,
                 send_sem=zs_sem.at[t, o - 1], recv_sem=zr_sem.at[t, o - 1],
-                device_id={"slab": gz_at * 8 + me}, device_id_type=MESH))
-        own = pltpu.make_async_copy(
-            zsend.at[t, zhi], planes.at[t, :, pl.ds(pl.multiple_of(zhi * BLOCK, 16), BLOCK), :],
-            local_sem.at[CHUNKS + t])
+                device_id={"state": (to % 2) * 4 + y, "slab": (to // 2) * 8 + me}, device_id_type=MESH))
+        own = pltpu.make_async_copy(zsend.at[t, spot], dst, local_sem.at[CHUNKS + t])
         return out_copies, own
 
     def y_copy(t):
@@ -215,17 +216,30 @@
     yc = [y_copy(t) for t in range(CHUNKS - 1)]
     start(xc[0])
 
+    row8 = lax.broadcasted_iota(jnp.int32, (8, 128), 0)
+    params[zlo] = jnp.where(row8 == 0, tilt, jnp.where(row8 == 1, lift, weight))
+    swap_params = pltpu.make_async_remote_copy(
+        src_ref=params.at[zlo], dst_ref=params.at[zlo], send_sem=ps_sem, recv_sem=pr_sem,
+        device_id={"state": (1 - zlo) * 4 + y}, device_id_type=MESH)
+    swap_params.start()
+    swap_params.wait()
+
     def tables(i, _):
-        rows = pl.ds(pl.multiple_of(i * 16, 16), 16)
-        row = lax.broadcasted_iota(jnp.int32, (16, PAD), 0) + i * 16
-        lane = lax.broadcasted_iota(jnp.int32, (16, PAD), 1)
-        cosine, sine = turn(centred(lane) * (tilt * (row.astype(f32) - centre)) * (1.0 / N))
-        cos_x[rows, :] = cosine
-        sin_x[rows, :] = sine
-        at = jnp.where(lane >= N, lane - 64, lane)
-        cosine, sine = turn(centred(row) * (lift * (at.astype(f32) - centre)) * (1.0 / N))
-        cos_z[rows, :] = cosine
-        sin_z[rows, :] = sine
+        row = (lax.broadcasted_iota(jnp.int32, (16, 128), 0) + i * 16)
+        for s in range(2):
+            rows = pl.ds(pl.multiple_of(s * N + i * 16, 16), 16)
+            tilt_s = params[s, 0:1, :]
+            lift_s = params[s, 1:2, :]
+            for tile in range(3):
+                lanes = slice(128 * tile, 128 * (tile + 1))
+                lane = lax.broadcasted_iota(jnp.int32, (16, 128), 1) + 128 * tile
+                cosine, sine = turn(centred(lane) * (tilt_s * (row.astype(f32) - centre)) * (1.0 / N))
+                cos_x[rows, lanes] = cosine
+                sin_x[rows, lanes] = sine
+                at = jnp.where(lane >= N, lane - 64, lane)
+                cosine, sine = turn(centred(row) * (lift_s * (at.astype(f32) - centre)) * (1.0 / N))
+                cos_z[rows, lanes] = cosine
+                sin_z[rows, lanes] = sine
         return 0
 
     lax.fori_loop(0, N // 16, tables, 0)
@@ -239,7 +253,7 @@
                     t, g, :, 128 * lane : 128 * (lane + 1)].astype(f32)
         for lane in range(5):
             for m in range(8):
-                zsend[t, m // 2, m % 2, :, 128 * lane : 128 * (lane + 1)] = turned[
+                zsend[t, m, :, 128 * lane : 128 * (lane + 1)] = turned[
                     lane, pl.ds(m, BLOCK, stride=8), :].astype(bf16)
 
     lane128 = lax.broadcasted_iota(jnp.int32, (N, 128), 1)
@@ -252,31 +266,35 @@
         return jnp.where(lane128 < 64, l, -l), jnp.where(lane128 < 64, r, -r)
 
     def shear_planes(t):
-        units = [((e, j), (e, 2 + j), j) for e in range(2) for j in range(2)] + [((0, 4), (1, 4), 2)]
-        for (ea, ta), (eb, tb), tile in units:
-            data = jnp.concatenate(
-                [planes[t, ea, :, 128 * ta : 128 * (ta + 1)], planes[t, eb, :, 128 * tb : 128 * (tb + 1)]], axis=1)
+        units = [((s, 2 * u), (s, 2 * u + 1), u) for u in range(2) for s in range(2)] + [((0, 4), (1, 4), 2)]
+        for sides in units:
+            tile = sides[2]
+            pair = sides[:2]
+            data = jnp.concatenate([planes[t, s, :, 128 * b : 128 * (b + 1)] for s, b in pair], axis=1)
             both = jnp.dot(fz[...], data, preferred_element_type=f32)
-            cosine = cos_z[:, 128 * tile : 128 * (tile + 1)]
-            sine = sin_z[:, 128 * tile : 128 * (tile + 1)]
             near, far = [], []
-            for s in range(2):
-                tc = both[:N, 128 * s : 128 * (s + 1)]
-                ts = both[N:, 128 * s : 128 * (s + 1)]
+            for i, (s, b) in enumerate(pair):
+                cosine = cos_z[s * N : (s + 1) * N, 128 * tile : 128 * (tile + 1)]
+                sine = sin_z[s * N : (s + 1) * N, 128 * tile : 128 * (tile + 1)]
+                tc = both[:N, 128 * i : 128 * (i + 1)]
+                ts = both[N:, 128 * i : 128 * (i + 1)]
                 near.append(cosine * tc - sine * ts)
                 far.append(cosine * ts + sine * tc)
             far = swap(far[0], far[1], tile < 2)
             ramped = jnp.concatenate([near[0] + far[0], near[1] + far[1]], axis=1).astype(bf16)
             both = jnp.dot(gz[...], ramped, preferred_element_type=f32)
             far = swap(both[N:, :128], both[N:, 128:], tile < 2)
-            second[ea, :, 128 * ta : 128 * (ta + 1)] = (both[:N, :128] - far[0]).astype(bf16)
-            second[eb, :, 128 * tb : 128 * (tb + 1)] = (both[:N, 128:] - far[1]).astype(bf16)
-        for e in range(2):
-            spectrum = jnp.dot(second[e], fwd3[...], preferred_element_type=f32)
-            re, im = spectrum[:, :PAD], spectrum[:, PAD:]
-            cosine, sine = cos_x[...], sin_x[...]
-            ramped = jnp.concatenate([re * cosine + im * sine, im * cosine - re * sine], axis=1).astype(bf16)
-            rsend[t, e] = (jnp.dot(ramped, inv[...], preferred_element_type=f32) * weight).astype(bf16)
+            for i, (s, b) in enumerate(pair):
+                second[s * N : (s + 1) * N, 128 * b : 128 * (b + 1)] = (
+                    both[:N, 128 * i : 128 * (i + 1)] - far[i]).astype(bf16)
+        spectrum = jnp.dot(second[...], fwd3[...], preferred_element_type=f32)
+        re, im = spectrum[:, :PAD], spectrum[:, PAD:]
+        cosine, sine = cos_x[...], sin_x[...]
+        ramped = jnp.concatenate([re * cosine + im * sine, im * cosine - re * sine], axis=1).astype(bf16)
+        moved = jnp.dot(ramped, inv[...], preferred_element_type=f32)
+        w0 = jnp.concatenate([params[0, 2:3, :]] * 5, axis=1)
+        w1 = jnp.concatenate([params[1, 2:3, :]] * 5, axis=1)
+        rsend[t] = (moved[:N] * w0 + moved[N:] * w1).astype(bf16)
 
     for t in range(CHUNKS):
         arrive(xc[t])
@@ -295,27 +313,24 @@
 
     def add(i, _):
         rows = pl.ds(pl.multiple_of(i * 16, 16), 16)
-        for e in range(2):
-            acc = rsend[CHUNKS - 1, e, rows, :].astype(f32)
-            for t in range(CHUNKS - 1):
-                acc = acc + rrecv[t, e, rows, :].astype(f32)
-            total[e, rows, :] = acc
+        acc = rsend[CHUNKS - 1, rows, :].astype(f32)
+        for t in range(CHUNKS - 1):
+            acc = acc + rrecv[t, rows, :].astype(f32)
+        total[rows, :] = acc
         return 0
 
     lax.fori_loop(0, N // 16, add, 0)
 
-    target = (x // 2) * 4 + y
-    slot = ((zlo * 2 + x % 2) * 4 + zhi) * 2 + core
-
-    packed[100:PACKED, :] = jnp.zeros((PACKED - 100, 128), f32)
+    target = core * 4 + y
+    slot = x * RING + spot
+
+    packed[FILLED:PACKED, :] = jnp.zeros((PACKED - FILLED, 128), f32)
 
     def pack(q, _):
         for i in range(4):
-            for e in range(2):
-                for b in range(5):
-                    rows = total[e, pl.ds(pl.multiple_of(q * 40, 8), 40), 128 * b : 128 * (b + 1)]
-                    at = (e * 5 + b) * 10
-                    packed[at : at + 10, :] = rows[10 * i : 10 * i + 10]
+            for b in range(5):
+                rows = total[pl.ds(pl.multiple_of(q * 40, 8), 40), 128 * b : 128 * (b + 1)]
+                packed[b * 10 : b * 10 + 10, :] = rows[10 * i : 10 * i + 10]
             fsend[q * 4 + i] = packed[...].astype(bf16)
         return 0
 
@@ -354,21 +369,18 @@
 
     lax.fori_loop(0, 32, land, 0)
 
-    for h in range(2):
-        for zz in range(4):
-            for coef in range(2):
-                at = (h * 4 + zz) * 2 + coef
-                packed[...] = frecv[at].astype(f32) + frecv[16 + at].astype(f32)
-                for e in range(2):
-                    row = 8 * h + 2 * zz + e
-                    for b in range(5):
-                        piece = packed[(e * 5 + b) * 10 : (e * 5 + b) * 10 + 10, :]
-                        base = coef * N + row
-                        if b < 4:
-                            final[b % 2, pl.ds(base + 16 * (b // 2), 10, stride=32), :] = piece
-                        else:
-                            final[2, pl.ds(base, 10, stride=32), :] = piece
-                            final[2, pl.ds(base + 16, 10, stride=32), :] = pltpu.roll(piece, 64, 1)
+    for coef in range(2):
+        for h in range(2):
+            for at in range(RING):
+                packed[...] = frecv[(coef * 2 + h) * RING + at].astype(f32)
+                for b in range(5):
+                    piece = packed[b * 10 : b * 10 + 10, :]
+                    base = coef * N + 8 * h + at
+                    if b < 4:
+                        final[b // 2, pl.ds(base + 16 * (b % 2), 10, stride=32), :] = piece
+                    else:
+                        final[2, pl.ds(base, 10, stride=32), :] = piece
+                        final[2, pl.ds(base + 16, 10, stride=32), :] = pltpu.roll(piece, 64, 1)
     out[:, 0:128] = final[0]
     out[:, 128:256] = final[1]
     out[:, 256:320] = final[2][:, :64]
@@ -397,23 +409,24 @@
         scratch_shapes=[
             vmem(image.shape, bf16), vmem(fwd.shape, bf16), vmem(inv.shape, bf16),
             vmem(fwd3.shape, bf16), vmem(fz.shape, bf16), vmem(gz.shape, bf16),
-            vmem((N, PAD), f32), vmem((N, PAD), f32), vmem((N, PAD), f32), vmem((N, PAD), f32),
+            vmem((2 * N, PAD), f32), vmem((2 * N, PAD), f32), vmem((2 * N, PAD), f32), vmem((2 * N, PAD), f32),
             vmem((8, 4, BLOCK, LANES), bf16),
             vmem((CHUNKS, 8, BLOCK, LANES), bf16),
-            vmem((CHUNKS, 4, 2, BLOCK, LANES), bf16),
+            vmem((CHUNKS, RING, BLOCK, LANES), bf16),
             vmem((CHUNKS, 2, N, LANES), bf16),
-            vmem((CHUNKS, 2, N, LANES), bf16),
-            vmem((CHUNKS - 1, 2, N, LANES), bf16),
+            vmem((CHUNKS, N, LANES), bf16),
+            vmem((CHUNKS - 1, N, LANES), bf16),
             vmem((32, PACKED, 128), bf16),
             vmem((32, PACKED, 128), bf16),
+            vmem((2, 8, 128), f32),
             vmem((5, 640, 128), f32),
-            vmem((2, N, LANES), bf16),
-            vmem((2, N, LANES), f32),
+            vmem((2 * N, LANES), bf16),
+            vmem((N, LANES), f32),
             vmem((PACKED, 128), f32),
             vmem((3, 640, 128), f32),
-            dma((6,)), dma((2 * CHUNKS,)),
+            dma((6,)), dma((2 * CHUNKS,)), dma, dma,
             dma((CHUNKS, 7)), dma((CHUNKS, 7)),
-            dma((CHUNKS, 3)), dma((CHUNKS, 3)),
+            dma((CHUNKS, RING - 1)), dma((CHUNKS, RING - 1)),
             dma((CHUNKS - 1,)), dma((CHUNKS - 1,)),
             dma((32,)), dma((32,)),
         ],

time: 161 us -> 128 us (0.80)
  Pallas kernels: 158 us -> 125 us
    pallas_call x1, Pallas kernels: 158 us -> 125 us  [body(): pl.pallas_call(kernel, name='shears', out_shape=jax.ShapeDtypeStruct((640...]
where the time goes in v2:
time: 128 us
  Pallas kernels  125 us (98%)
  local copies, waits for them, and re-layouts  2.22 us (2%)
  between operations  1.31 us (1%)
    pallas_call x1, Pallas kernels, body(): pl.pallas_call(kernel, name='shears', out_shape=jax.ShapeDtypeStruct((640...  125 us

profile of v2, /device:TPU:15, one launch (start us, length us, event | category | flops | bytes accessed | tf_op | source)
XLA Modules:
  0.0 128.1 jit_solution(9542187438295280593)
XLA Ops:
  1.3 124.6 %shears.1 = f32[640,320]{1,0:T(8,128)} custom-call(s32[1]{0:T(128)S(6)} %copy.11.rot, s32[1]{0:T(128)S(6)} %copy.12.counts, f32[2,32]{1,0:T(2,128)} %constant.17.clone.shifts, bf16[2,10,640,128]{3,2,1,0:T(8,128)(2,1)} %bitcast.5, bf16[640,768]{1,0:T(8,128)(2,1)} %constant.12.clone.fwd_hbm, bf16[768,640]{1,0:T(8,128)(2,1)} %constant.13.clone.inv_hbm, ...), custom_call_target="tpu_custom_call" | custom-call | flops 12999999488 | bytes 8000000 | tf_op jit(solution)/shard_map/shears/pallas_call | solution.py:403
  125.9 2.2 %copy.13 = f32[2,10,2,320,16]{3,4,2,1,0:T(8,128)} copy(f32[2,10,2,320,16]{3,4,2,1,0:T(8,128)} %bitcast.4) | data formatting | bytes 1638400

commit v3 on v2

v3 whole, which is shorter than its diff:
```python
import math

import jax
import jax.numpy as jnp
import numpy as np
from jax import lax
from jax.experimental import pallas as pl
from jax.experimental.pallas import tpu as pltpu
from jax.sharding import PartitionSpec as P

N = 320
HALF = N // 2
ANGLES = 32
LANES = 640
PAD = 384
WIDE = 2 * PAD
BLOCK = 80
CHUNKS = 4
PACKED = 64
FILLED = 50
RING = 8
MESH = pl.DeviceIdType.MESH
f32 = jnp.float32
bf16 = jnp.bfloat16


def packed_lane(part, x):
    return np.where(x < 256, x // 128 * 256 + part * 128 + x % 128, 512 + part * 64 + (x - 256))


def host_tables():
    points = np.arange(N)
    phase = (points[:, None] * points[None, :] % N) * (2.0 * math.pi / N)
    cosine = np.cos(phase)
    sine = np.sin(phase)
    forward = np.zeros((2, N, 2, PAD))
    forward[0, :, 0, :N] = cosine
    forward[1, :, 0, :N] = sine
    forward[0, :, 1, :N] = -sine
    forward[1, :, 1, :N] = cosine
    forward = forward.reshape(2 * N, WIDE)
    inverse = np.zeros((2, PAD, 2, N))
    inverse[0, :N, 0] = cosine / N
    inverse[1, :N, 0] = -sine / N
    inverse[0, :N, 1] = sine / N
    inverse[1, :N, 1] = cosine / N
    inverse = inverse.reshape(WIDE, 2 * N)
    order = np.zeros(2 * N, np.int64)
    for part in range(2):
        order[packed_lane(part, points)] = part * N + points
    angle = -(np.arange(ANGLES) - ANGLES // 2) * math.pi / 120.0
    shifts = np.stack([-np.tan(angle / 2.0), np.sin(angle)])
    return (
        jnp.asarray(forward.astype(jnp.bfloat16)),
        jnp.asarray(inverse[:, order].astype(jnp.bfloat16)),
        jnp.asarray(forward[order].astype(jnp.bfloat16)),
        jnp.asarray(np.concatenate([cosine, sine]).astype(jnp.bfloat16)),
        jnp.asarray((np.concatenate([cosine, sine]) / N).astype(jnp.bfloat16)),
        jnp.asarray(shifts.astype(np.float32)),
    )


def turn(turns):
    half = (turns - jnp.floor(turns + 0.5)) * math.pi
    sq = half * half
    s = -1.0 / 39916800.0
    for c in (1.0 / 362880.0, -1.0 / 5040.0, 1.0 / 120.0, -1.0 / 6.0, 1.0):
        s = s * sq + c
    s = s * half
    c = 1.0 / 479001600.0
    for k in (-1.0 / 3628800.0, 1.0 / 40320.0, -1.0 / 720.0, 1.0 / 24.0, -0.5, 1.0):
        c = c * sq + k
    return 1.0 - 2.0 * s * s, 2.0 * s * c


def centred(index):
    return jnp.where(index >= HALF, index - N, index).astype(f32)


def unit_lanes(u):
    return slice(256 * u, 256 * u + (256 if u < 2 else 128))


def kernel(
    rot_hbm, counts_hbm, shifts, image, fwd_hbm, inv_hbm, fwd3_hbm, fz_hbm, gz_hbm,
    out,
    rot, counts, v, vt, fwd, inv, fwd3, fz, gz,
    cos_f, sin_f, cos_x, sin_x, cos_z, sin_z,
    xsend, xrecv, zsend, planes, rsend, rrecv, fsend, frecv,
    params, turned, second, total, packed, final,
    image_sem, load_sem, xl_sem, zl_sem, ps_sem, pr_sem,
    xs_sem, xr_sem, zs_sem, zr_sem, ys_sem, yr_sem, fs_sem, fr_sem,
):
    state = lax.axis_index("state")
    slab = lax.axis_index("slab")
    zlo = state // 4
    y = state % 4
    zhi = slab // 8
    x = (slab % 8) // 2
    core = slab % 2
    me = slab % 8
    spot = zhi * 2 + zlo

    def image_load(i):
        part = pl.ds(2 * i, 2)
        return pltpu.make_async_copy(image.at[:, part], v.at[:, part], image_sem.at[i])

    loads = [
        pltpu.make_async_copy(src, dst, load_sem.at[i])
        for i, (src, dst) in enumerate(
            ((rot_hbm, rot), (counts_hbm, counts), (fwd_hbm, fwd), (inv_hbm, inv),
             (fz_hbm, fz), (gz_hbm, gz), (fwd3_hbm, fwd3))
        )
    ]
    for copy in loads[:2]:
        copy.start()
    for i in range(5):
        image_load(i).start()
    for copy in loads[2:]:
        copy.start()

    barrier = pltpu.get_barrier_semaphore()

    def greet(i, _):
        at = lax.rem(zlo * 32 + slab + i, 64)
        pl.semaphore_signal(
            barrier, inc=1,
            device_id={"state": (at // 32) * 4 + y, "slab": lax.rem(at, 32)},
            device_id_type=MESH,
        )
        return 0

    lax.fori_loop(1, 64, greet, 0)
    for i in range(1, 4):
        pl.semaphore_signal(
            barrier, inc=1,
            device_id={"state": zlo * 4 + lax.rem(y + i, 4), "slab": slab},
            device_id_type=MESH,
        )

    for copy in loads[:2]:
        copy.wait()
    tilt = shifts[0, rot[0]]
    lift = shifts[1, rot[0]]
    weight = counts[0].astype(f32) * (1.0 / 64.0)
    centre = (N - 1) / 2.0

    row = lax.broadcasted_iota(jnp.int32, (16, PAD), 0) + slab * 10
    freq = centred(lax.broadcasted_iota(jnp.int32, (16, PAD), 1)) * (1.0 / N)
    cosine, sine = turn(freq * (tilt * (row.astype(f32) - centre)))
    cos_f[...] = cosine
    sin_f[...] = sine

    row8 = lax.broadcasted_iota(jnp.int32, (8, 128), 0)
    params[zlo] = jnp.where(row8 == 0, tilt, jnp.where(row8 == 1, lift, weight))
    swap_params = pltpu.make_async_remote_copy(
        src_ref=params.at[zlo], dst_ref=params.at[zlo], send_sem=ps_sem, recv_sem=pr_sem,
        device_id={"state": (1 - zlo) * 4 + y}, device_id_type=MESH)

    def turn_image(i, _):
        image_load(i).wait()
        for coef in range(2):
            for j in range(2):
                vt[coef, 2 * i + j] = v[coef, 2 * i + j].T
        return 0

    lax.fori_loop(0, 5, turn_image, 0)
    for copy in loads[2:4]:
        copy.wait()

    def chunk_y(t):
        return lax.rem(y + 1 + t, 4)

    def first(t):
        yy = chunk_y(t)
        left = jnp.concatenate(
            [vt[coef, z, pl.ds(pl.multiple_of(64 * low + 16 * yy, 16), 16), :]
             for z in range(10) for coef in range(2) for low in range(2)], axis=0)
        spectrum = jnp.dot(left, fwd[...], preferred_element_type=f32)
        ramped = []
        for z in range(10):
            cosine = jnp.broadcast_to(cos_f[z : z + 1, :], (64, PAD))
            sine = jnp.broadcast_to(sin_f[z : z + 1, :], (64, PAD))
            re = spectrum[64 * z : 64 * (z + 1), :PAD]
            im = spectrum[64 * z : 64 * (z + 1), PAD:]
            ramped.append(
                jnp.concatenate([re * cosine + im * sine, im * cosine - re * sine], axis=1).astype(bf16))
        moved = jnp.dot(jnp.concatenate(ramped, axis=0), inv[...], preferred_element_type=f32)
        for pair in range(5):
            for coef in range(2):
                for low in range(2):
                    for h in range(2):
                        q = 128 * pair + 32 * coef + 16 * low + 8 * h
                        piece = jnp.concatenate([moved[q : q + 8], moved[q + 64 : q + 72]], axis=0)
                        xsend[(coef * 2 + h) * 2 + low, t, 16 * pair : 16 * (pair + 1), :] = piece.astype(bf16)

    def x_copies(t, u):
        lanes = unit_lanes(u)
        lanes = pl.ds(lanes.start, lanes.stop - lanes.start)
        out_copies = []
        for o in range(1, 8):
            gx = lax.rem(x + o // 2, 4)
            gc = lax.rem(core + o, 2)
            out_copies.append(pltpu.make_async_remote_copy(
                src_ref=xsend.at[gx * 2 + gc, t, :, lanes], dst_ref=xrecv.at[t, me, :, lanes],
                send_sem=xs_sem.at[t, u, o - 1], recv_sem=xr_sem.at[t, u, o - 1],
                device_id={"slab": zhi * 8 + gx * 2 + gc}, device_id_type=MESH))
        own = pltpu.make_async_copy(
            xsend.at[me, t, :, lanes], xrecv.at[t, me, :, lanes], xl_sem.at[t, u])
        return out_copies, own

    def z_copies(t, u):
        lanes = unit_lanes(u)
        lanes = pl.ds(lanes.start, lanes.stop - lanes.start)
        out_copies = []
        dst = planes.at[t, zlo, pl.ds(pl.multiple_of(zhi * BLOCK, 16), BLOCK), lanes]
        for o in (4, 3, 5, 2, 6, 1, 7):
            to = lax.rem(spot + o, RING)
            out_copies.append(pltpu.make_async_remote_copy(
                src_ref=zsend.at[t, to, :, lanes], dst_ref=dst,
                send_sem=zs_sem.at[t, u, o - 1], recv_sem=zr_sem.at[t, u, o - 1],
                device_id={"state": (to % 2) * 4 + y, "slab": (to // 2) * 8 + me}, device_id_type=MESH))
        own = pltpu.make_async_copy(zsend.at[t, spot, :, lanes], dst, zl_sem.at[t, u])
        return out_copies, own

    def y_copy(t):
        return pltpu.make_async_remote_copy(
            src_ref=rsend.at[t], dst_ref=rrecv.at[t],
            send_sem=ys_sem.at[t], recv_sem=yr_sem.at[t],
            device_id={"state": zlo * 4 + chunk_y(t)}, device_id_type=MESH)

    def start(copies):
        remote, own = copies
        for copy in remote:
            copy.start()
        own.start()

    def arrive(copies):
        remote, own = copies
        own.wait()
        for copy in remote:
            copy.wait_recv()

    first(0)
    pl.semaphore_wait(barrier, 66)
    start(x_copies(0, 0))
    swap_params.start()
    start(x_copies(0, 1))
    start(x_copies(0, 2))
    for copy in loads[4:]:
        copy.wait()
    swap_params.wait()

    def tables(i, _):
        row = lax.broadcasted_iota(jnp.int32, (16, 128), 0) + i * 16
        for s in range(2):
            rows = pl.ds(pl.multiple_of(s * N + i * 16, 16), 16)
            tilt_s = params[s, 0:1, :]
            lift_s = params[s, 1:2, :]
            for tile in range(3):
                lanes = slice(128 * tile, 128 * (tile + 1))
                lane = lax.broadcasted_iota(jnp.int32, (16, 128), 1) + 128 * tile
                cosine, sine = turn(centred(lane) * (tilt_s * (row.astype(f32) - centre)) * (1.0 / N))
                cos_x[rows, lanes] = cosine
                sin_x[rows, lanes] = sine
                at = jnp.where(lane >= N, lane - 64, lane)
                cosine, sine = turn(centred(row) * (lift_s * (at.astype(f32) - centre)) * (1.0 / N))
                cos_z[rows, lanes] = cosine
                sin_z[rows, lanes] = sine
        return 0

    def transpose(t, u):
        lanes = unit_lanes(u)
        for lane in range(lanes.start // 128, lanes.stop // 128):
            for g in range(8):
                turned[lane, BLOCK * g : BLOCK * (g + 1), :] = xrecv[
                    t, g, :, 128 * lane : 128 * (lane + 1)].astype(f32)
        for lane in range(lanes.start // 128, lanes.stop // 128):
            for m in range(8):
                zsend[t, m, :, 128 * lane : 128 * (lane + 1)] = turned[
                    lane, pl.ds(m, BLOCK, stride=8), :].astype(bf16)

    lane128 = lax.broadcasted_iota(jnp.int32, (N, 128), 1)

    def swap(left, right, paired):
        if paired:
            return right, -left
        l = pltpu.roll(left, 64, 1)
        r = pltpu.roll(right, 64, 1)
        return jnp.where(lane128 < 64, l, -l), jnp.where(lane128 < 64, r, -r)

    def shear_z(t, u):
        if u < 2:
            pairs = [((s, 2 * u), (s, 2 * u + 1)) for s in range(2)]
        else:
            pairs = [((0, 4), (1, 4))]
        for pair in pairs:
            data = jnp.concatenate([planes[t, s, :, 128 * b : 128 * (b + 1)] for s, b in pair], axis=1)
            both = jnp.dot(fz[...], data, preferred_element_type=f32)
            near, far = [], []
            for i, (s, b) in enumerate(pair):
                cosine = cos_z[s * N : (s + 1) * N, 128 * u : 128 * (u + 1)]
                sine = sin_z[s * N : (s + 1) * N, 128 * u : 128 * (u + 1)]
                tc = both[:N, 128 * i : 128 * (i + 1)]
                ts = both[N:, 128 * i : 128 * (i + 1)]
                near.append(cosine * tc - sine * ts)
                far.append(cosine * ts + sine * tc)
            far = swap(far[0], far[1], u < 2)
            ramped = jnp.concatenate([near[0] + far[0], near[1] + far[1]], axis=1).astype(bf16)
            both = jnp.dot(gz[...], ramped, preferred_element_type=f32)
            far = swap(both[N:, :128], both[N:, 128:], u < 2)
            for i, (s, b) in enumerate(pair):
                second[s * N : (s + 1) * N, 128 * b : 128 * (b + 1)] = (
                    both[:N, 128 * i : 128 * (i + 1)] - far[i]).astype(bf16)

    def shear_x(t):
        spectrum = jnp.dot(second[...], fwd3[...], preferred_element_type=f32)
        re, im = spectrum[:, :PAD], spectrum[:, PAD:]
        cosine, sine = cos_x[...], sin_x[...]
        ramped = jnp.concatenate([re * cosine + im * sine, im * cosine - re * sine], axis=1).astype(bf16)
        moved = jnp.dot(ramped, inv[...], preferred_element_type=f32)
        w0 = jnp.concatenate([params[0, 2:3, :]] * 5, axis=1)
        w1 = jnp.concatenate([params[1, 2:3, :]] * 5, axis=1)
        rsend[t] = (moved[:N] * w0 + moved[N:] * w1).astype(bf16)

    def step(t, _):
        @pl.when(t < CHUNKS - 1)
        def _():
            first(t + 1)

        @pl.when(t < CHUNKS)
        def _():
            for u in range(3):
                arrive(x_copies(t, u))
                transpose(t, u)
                start(z_copies(t, u))

                @pl.when(t < CHUNKS - 1)
                def _():
                    start(x_copies(t + 1, u))

        @pl.when(t == 0)
        def _():
            lax.fori_loop(0, N // 16, tables, 0)

        @pl.when(t >= 1)
        def _():
            for u in range(3):
                arrive(z_copies(t - 1, u))
                shear_z(t - 1, u)
            shear_x(t - 1)

            @pl.when(t < CHUNKS)
            def _():
                y_copy(t - 1).start()

        return 0

    lax.fori_loop(0, CHUNKS + 1, step, 0)
    for t in range(CHUNKS - 1):
        y_copy(t).wait_recv()

    def add(i, _):
        rows = pl.ds(pl.multiple_of(i * 16, 16), 16)
        acc = rsend[CHUNKS - 1, rows, :].astype(f32)
        for t in range(CHUNKS - 1):
            acc = acc + rrecv[t, rows, :].astype(f32)
        total[rows, :] = acc
        return 0

    lax.fori_loop(0, N // 16, add, 0)

    target = core * 4 + y
    slot = x * RING + spot
    packed[FILLED:PACKED, :] = jnp.zeros((PACKED - FILLED, 128), f32)

    def f_copy(to):
        return pltpu.make_async_remote_copy(
            src_ref=fsend.at[to], dst_ref=frecv.at[slot],
            send_sem=fs_sem.at[to], recv_sem=fr_sem.at[slot],
            device_id={"state": target, "slab": to}, device_id_type=MESH)

    def is_own(to):
        return jnp.logical_and(to == slab, target == state)

    def pack(i, _):
        q = lax.rem(slab // 4 + 4 + i, 8)
        for i in range(4):
            to = q * 4 + i
            for b in range(5):
                rows = total[pl.ds(pl.multiple_of(q * 40, 8), 40), 128 * b : 128 * (b + 1)]
                packed[b * 10 : b * 10 + 10, :] = rows[10 * i : 10 * i + 10]
            fsend[to] = packed[...].astype(bf16)

            @pl.when(is_own(to))
            def _():
                pltpu.make_async_copy(fsend.at[slab], frecv.at[slot], fr_sem.at[slot]).start()

            @pl.when(jnp.logical_not(is_own(to)))
            def _():
                f_copy(to).start()

        return 0

    lax.fori_loop(0, 8, pack, 0)

    def sent(t, _):
        for u in range(3):
            for copy in x_copies(t, u)[0] + z_copies(t, u)[0]:
                copy.wait_send()
        return 0

    lax.fori_loop(0, CHUNKS, sent, 0)
    for t in range(CHUNKS - 1):
        y_copy(t).wait_send()

    for coef in range(2):
        for h in range(2):
            for at in range(RING):
                i = (coef * 2 + h) * RING + at
                pltpu.make_async_copy(fsend.at[0], frecv.at[i], fr_sem.at[i]).wait()
                packed[...] = frecv[i].astype(f32)
                for b in range(5):
                    piece = packed[b * 10 : b * 10 + 10, :]
                    base = coef * N + 8 * h + at
                    if b < 4:
                        final[b // 2, pl.ds(base + 16 * (b % 2), 10, stride=32), :] = piece
                    else:
                        final[2, pl.ds(base, 10, stride=32), :] = piece
                        final[2, pl.ds(base + 16, 10, stride=32), :] = pltpu.roll(piece, 64, 1)
    out[:, 0:128] = final[0]
    out[:, 128:256] = final[1]
    out[:, 256:320] = final[2][:, :64]

    def left(to, _):
        @pl.when(jnp.logical_not(is_own(to)))
        def _():
            f_copy(to).wait_send()

        return 0

    lax.fori_loop(0, 32, left, 0)


def body(state_images, rot_index, counts):
    fwd, inv, fwd3, fz, gz, shifts = host_tables()
    image = state_images.reshape(2, 10, 2 * N, 128)
    smem = pl.BlockSpec(memory_space=pltpu.SMEM)
    anywhere = pl.BlockSpec(memory_space=pl.ANY)
    dma = pltpu.SemaphoreType.DMA
    vmem = pltpu.VMEM
    out = pl.pallas_call(
        kernel,
        name="shears",
        out_shape=jax.ShapeDtypeStruct((640, N), f32),
        in_specs=[anywhere, anywhere, smem] + [anywhere] * 6,
        out_specs=pl.BlockSpec(memory_space=vmem),
        scratch_shapes=[
            pltpu.SMEM((1,), jnp.int32), pltpu.SMEM((1,), jnp.int32),
            vmem(image.shape, bf16), vmem((2, 10, 128, LANES), bf16), vmem(fwd.shape, bf16), vmem(inv.shape, bf16),
            vmem(fwd3.shape, bf16), vmem(fz.shape, bf16), vmem(gz.shape, bf16),
            vmem((16, PAD), f32), vmem((16, PAD), f32),
            vmem((2 * N, PAD), f32), vmem((2 * N, PAD), f32), vmem((2 * N, PAD), f32), vmem((2 * N, PAD), f32),
            vmem((8, 4, BLOCK, LANES), bf16),
            vmem((CHUNKS, 8, BLOCK, LANES), bf16),
            vmem((CHUNKS, RING, BLOCK, LANES), bf16),
            vmem((CHUNKS, 2, N, LANES), bf16),
            vmem((CHUNKS, N, LANES), bf16),
            vmem((CHUNKS - 1, N, LANES), bf16),
            vmem((32, PACKED, 128), bf16),
            vmem((32, PACKED, 128), bf16),
            vmem((2, 8, 128), f32),
            vmem((5, 640, 128), f32),
            vmem((2 * N, LANES), bf16),
            vmem((N, LANES), f32),
            vmem((PACKED, 128), f32),
            vmem((3, 640, 128), f32),
            dma((5,)), dma((7,)), dma((CHUNKS, 3)), dma((CHUNKS, 3)), dma, dma,
            dma((CHUNKS, 3, 7)), dma((CHUNKS, 3, 7)),
            dma((CHUNKS, 3, RING - 1)), dma((CHUNKS, 3, RING - 1)),
            dma((CHUNKS - 1,)), dma((CHUNKS - 1,)),
            dma((32,)), dma((32,)),
        ],
        compiler_params=pltpu.CompilerParams(
            collective_id=0, has_side_effects=True, vmem_limit_bytes=60 * 1024 * 1024),
        cost_estimate=pl.CostEstimate(flops=13_000_000_000, bytes_accessed=8_000_000, transcendentals=0),
    )(rot_index, counts, shifts, image, fwd, inv, fwd3, fz, gz)
    return out.reshape(2, 10, 2, 16, N).swapaxes(3, 4)


def solution(mesh):
    placed = (P("state", None, "slab", None, None, None), P("state"), P("state"))
    return jax.shard_map(
        body,
        mesh=mesh,
        in_specs=placed,
        out_specs=P(None, "slab", None, None, "state"),
        check_vma=False,
    )
```

time: 128 us -> 120 us (0.938)
  Pallas kernels: 125 us -> 116 us
    pallas_call x1, Pallas kernels: 125 us -> 116 us  [body(): pl.pallas_call(kernel, name='shears', out_shape=jax.ShapeDtypeStruct((640...]
where the time goes in v3:
time: 120 us; the launch traced here: 119 us
  Pallas kernels  116 us (97%)
  local copies, waits for them, and re-layouts  2.22 us (2%)
  between operations  1.3 us (1%)
    pallas_call x1, Pallas kernels, body(): pl.pallas_call(kernel, name='shears', out_shape=jax.ShapeDtypeStruct((640...  116 us

profile of v3, /device:TPU:15, one launch (start us, length us, event | category | flops | bytes accessed | tf_op | source)
XLA Modules:
  0.0 119.3 jit_solution(986141847907540523)
XLA Ops:
  1.3 115.8 %shears.1 = f32[640,320]{1,0:T(8,128)} custom-call(s32[1]{0:T(128)S(6)} %copy.11.rot_hbm, s32[1]{0:T(128)S(6)} %copy.12.counts_hbm, f32[2,32]{1,0:T(2,128)} %constant.17.clone.shifts, bf16[2,10,640,128]{3,2,1,0:T(8,128)(2,1)} %bitcast.5, bf16[640,768]{1,0:T(8,128)(2,1)} %constant.12.clone.fwd_hbm, bf16[768,640]{1,0:T(8,128)(2,1)} %constant.13.clone.inv_hbm, ...), custom_call_target="tpu_custom_call" | custom-call | flops 12999999488 | bytes 8000000 | tf_op jit(solution)/shard_map/shears/pallas_call | solution.py:452
  117.1 2.2 %copy.13 = f32[2,10,2,320,16]{3,4,2,1,0:T(8,128)} copy(f32[2,10,2,320,16]{3,4,2,1,0:T(8,128)} %bitcast.4) | data formatting | bytes 1638400

commit v4 on v3

--- a/solution.py
+++ b/solution.py
@@ -16,6 +16,7 @@
 WIDE = 2 * PAD
 BLOCK = 80
 CHUNKS = 4
+UNITS = (2, 0, 1)
 PACKED = 64
 FILLED = 50
 RING = 8
@@ -116,27 +117,26 @@
         copy.start()
     for i in range(5):
         image_load(i).start()
+
+    barrier = pltpu.get_barrier_semaphore()
+
+    def greet(i, _):
+        to = lax.rem(slab + i, 32)
+        for other in range(2):
+            pl.semaphore_signal(
+                barrier, inc=1,
+                device_id={"state": other * 4 + y, "slab": to},
+                device_id_type=MESH,
+            )
+        return 0
+
+    lax.fori_loop(1, 32, greet, 0)
+    pl.semaphore_signal(barrier, inc=1, device_id={"state": (1 - zlo) * 4 + y}, device_id_type=MESH)
+    for i in range(1, 4):
+        pl.semaphore_signal(
+            barrier, inc=1, device_id={"state": zlo * 4 + lax.rem(y + i, 4)}, device_id_type=MESH)
     for copy in loads[2:]:
         copy.start()
-
-    barrier = pltpu.get_barrier_semaphore()
-
-    def greet(i, _):
-        at = lax.rem(zlo * 32 + slab + i, 64)
-        pl.semaphore_signal(
-            barrier, inc=1,
-            device_id={"state": (at // 32) * 4 + y, "slab": lax.rem(at, 32)},
-            device_id_type=MESH,
-        )
-        return 0
-
-    lax.fori_loop(1, 64, greet, 0)
-    for i in range(1, 4):
-        pl.semaphore_signal(
-            barrier, inc=1,
-            device_id={"state": zlo * 4 + lax.rem(y + i, 4), "slab": slab},
-            device_id_type=MESH,
-        )
 
     for copy in loads[:2]:
         copy.wait()
@@ -205,9 +205,8 @@
                 src_ref=xsend.at[gx * 2 + gc, t, :, lanes], dst_ref=xrecv.at[t, me, :, lanes],
                 send_sem=xs_sem.at[t, u, o - 1], recv_sem=xr_sem.at[t, u, o - 1],
                 device_id={"slab": zhi * 8 + gx * 2 + gc}, device_id_type=MESH))
-        own = pltpu.make_async_copy(
+        return out_copies, lambda: pltpu.make_async_copy(
             xsend.at[me, t, :, lanes], xrecv.at[t, me, :, lanes], xl_sem.at[t, u])
-        return out_copies, own
 
     def z_copies(t, u):
         lanes = unit_lanes(u)
@@ -220,8 +219,7 @@
                 src_ref=zsend.at[t, to, :, lanes], dst_ref=dst,
                 send_sem=zs_sem.at[t, u, o - 1], recv_sem=zr_sem.at[t, u, o - 1],
                 device_id={"state": (to % 2) * 4 + y, "slab": (to // 2) * 8 + me}, device_id_type=MESH))
-        own = pltpu.make_async_copy(zsend.at[t, spot, :, lanes], dst, zl_sem.at[t, u])
-        return out_copies, own
+        return out_copies, lambda: pltpu.make_async_copy(zsend.at[t, spot, :, lanes], dst, zl_sem.at[t, u])
 
     def y_copy(t):
         return pltpu.make_async_remote_copy(
@@ -233,20 +231,19 @@
         remote, own = copies
         for copy in remote:
             copy.start()
-        own.start()
+        own().start()
 
     def arrive(copies):
         remote, own = copies
-        own.wait()
+        own().wait()
         for copy in remote:
             copy.wait_recv()
 
     first(0)
     pl.semaphore_wait(barrier, 66)
-    start(x_copies(0, 0))
+    start(x_copies(0, UNITS[0]))
     swap_params.start()
-    start(x_copies(0, 1))
-    start(x_copies(0, 2))
+    start(x_copies(0, UNITS[1]))
     for copy in loads[4:]:
         copy.wait()
     swap_params.wait()
@@ -324,16 +321,20 @@
         rsend[t] = (moved[:N] * w0 + moved[N:] * w1).astype(bf16)
 
     def step(t, _):
-        @pl.when(t < CHUNKS - 1)
-        def _():
-            first(t + 1)
-
         @pl.when(t < CHUNKS)
         def _():
-            for u in range(3):
+            for i, u in enumerate(UNITS):
                 arrive(x_copies(t, u))
                 transpose(t, u)
                 start(z_copies(t, u))
+                if i == 0:
+                    @pl.when(t == 0)
+                    def _():
+                        start(x_copies(0, UNITS[2]))
+
+                    @pl.when(t < CHUNKS - 1)
+                    def _():
+                        first(t + 1)
 
                 @pl.when(t < CHUNKS - 1)
                 def _():
@@ -345,7 +346,7 @@
 
         @pl.when(t >= 1)
         def _():
-            for u in range(3):
+            for u in UNITS:
                 arrive(z_copies(t - 1, u))
                 shear_z(t - 1, u)
             shear_x(t - 1)

time: 120 us -> 118 us (0.983)
  Pallas kernels: 116 us -> 114 us
    pallas_call x1, Pallas kernels: 116 us -> 114 us  [body(): pl.pallas_call(kernel, name='shears', out_shape=jax.ShapeDtypeStruct((640...]
where the time goes in v4:
time: 118 us
  Pallas kernels  114 us (97%)
  local copies, waits for them, and re-layouts  2.22 us (2%)
  between operations  1.3 us (1%)
    pallas_call x1, Pallas kernels, body(): pl.pallas_call(kernel, name='shears', out_shape=jax.ShapeDtypeStruct((640...  114 us

profile of v4, /device:TPU:15, one launch (start us, length us, event | category | flops | bytes accessed | tf_op | source)
XLA Modules:
  0.0 117.5 jit_solution(9096714528885915610)
XLA Ops:
  1.3 114.0 %shears.1 = f32[640,320]{1,0:T(8,128)} custom-call(s32[1]{0:T(128)S(6)} %copy.11.rot_hbm, s32[1]{0:T(128)S(6)} %copy.12.counts_hbm, f32[2,32]{1,0:T(2,128)} %constant.17.clone.shifts, bf16[2,10,640,128]{3,2,1,0:T(8,128)(2,1)} %bitcast.5, bf16[640,768]{1,0:T(8,128)(2,1)} %constant.12.clone.fwd_hbm, bf16[768,640]{1,0:T(8,128)(2,1)} %constant.13.clone.inv_hbm, ...), custom_call_target="tpu_custom_call" | custom-call | flops 12999999488 | bytes 8000000 | tf_op jit(solution)/shard_map/shears/pallas_call | solution.py:453
  115.3 2.2 %copy.13 = f32[2,10,2,320,16]{3,4,2,1,0:T(8,128)} copy(f32[2,10,2,320,16]{3,4,2,1,0:T(8,128)} %bitcast.4) | data formatting | bytes 1638400

commit v5 on v4

--- a/solution.py
+++ b/solution.py
@@ -89,7 +89,7 @@
     cos_f, sin_f, cos_x, sin_x, cos_z, sin_z,
     xsend, xrecv, zsend, planes, rsend, rrecv, fsend, frecv,
     params, turned, second, total, packed, final,
-    image_sem, load_sem, xl_sem, zl_sem, ps_sem, pr_sem,
+    ready, image_sem, load_sem, xl_sem, zl_sem, ps_sem, pr_sem,
     xs_sem, xr_sem, zs_sem, zr_sem, ys_sem, yr_sem, fs_sem, fr_sem,
 ):
     state = lax.axis_index("state")
@@ -120,22 +120,19 @@
 
     barrier = pltpu.get_barrier_semaphore()
 
-    def greet(i, _):
-        to = lax.rem(slab + i, 32)
-        for other in range(2):
-            pl.semaphore_signal(
-                barrier, inc=1,
-                device_id={"state": other * 4 + y, "slab": to},
-                device_id_type=MESH,
-            )
-        return 0
-
-    lax.fori_loop(1, 32, greet, 0)
-    pl.semaphore_signal(barrier, inc=1, device_id={"state": (1 - zlo) * 4 + y}, device_id_type=MESH)
-    for i in range(1, 4):
+    def ring(o):
+        to = lax.rem(spot + o, RING)
+        return {"state": (to % 2) * 4 + y, "slab": (to // 2) * 8 + me}
+
+    for o in range(1, 8):
         pl.semaphore_signal(
-            barrier, inc=1, device_id={"state": zlo * 4 + lax.rem(y + i, 4)}, device_id_type=MESH)
-    for copy in loads[2:]:
+            barrier, inc=1, device_id={"slab": zhi * 8 + lax.rem(me + o, 8)}, device_id_type=MESH)
+    for o in range(1, RING):
+        pl.semaphore_signal(barrier, inc=1, device_id=ring(o), device_id_type=MESH)
+    for o in range(1, 4):
+        pl.semaphore_signal(
+            barrier, inc=1, device_id={"state": zlo * 4 + lax.rem(y + o, 4)}, device_id_type=MESH)
+    for copy in loads[2:4]:
         copy.start()
 
     for copy in loads[:2]:
@@ -240,13 +237,14 @@
             copy.wait_recv()
 
     first(0)
-    pl.semaphore_wait(barrier, 66)
+    pl.semaphore_wait(barrier, 2 * 7 + 3)
     start(x_copies(0, UNITS[0]))
     swap_params.start()
     start(x_copies(0, UNITS[1]))
+    for o in range(1, RING):
+        pl.semaphore_signal(ready, inc=1, device_id=ring(o), device_id_type=MESH)
     for copy in loads[4:]:
-        copy.wait()
-    swap_params.wait()
+        copy.start()
 
     def tables(i, _):
         row = lax.broadcasted_iota(jnp.int32, (16, 128), 0) + i * 16
@@ -342,6 +340,9 @@
 
         @pl.when(t == 0)
         def _():
+            swap_params.wait()
+            for copy in loads[4:]:
+                copy.wait()
             lax.fori_loop(0, N // 16, tables, 0)
 
         @pl.when(t >= 1)
@@ -361,19 +362,10 @@
     for t in range(CHUNKS - 1):
         y_copy(t).wait_recv()
 
-    def add(i, _):
-        rows = pl.ds(pl.multiple_of(i * 16, 16), 16)
-        acc = rsend[CHUNKS - 1, rows, :].astype(f32)
-        for t in range(CHUNKS - 1):
-            acc = acc + rrecv[t, rows, :].astype(f32)
-        total[rows, :] = acc
-        return 0
-
-    lax.fori_loop(0, N // 16, add, 0)
-
     target = core * 4 + y
     slot = x * RING + spot
-    packed[FILLED:PACKED, :] = jnp.zeros((PACKED - FILLED, 128), f32)
+    for g in range(8):
+        packed[g, FILLED:PACKED, :] = jnp.zeros((PACKED - FILLED, 128), f32)
 
     def f_copy(to):
         return pltpu.make_async_remote_copy(
@@ -385,13 +377,19 @@
         return jnp.logical_and(to == slab, target == state)
 
     def pack(i, _):
-        q = lax.rem(slab // 4 + 4 + i, 8)
-        for i in range(4):
-            to = q * 4 + i
+        block = lax.rem(zhi + 2 + i, 4)
+        rows = pl.ds(pl.multiple_of(block * BLOCK, 16), BLOCK)
+        for b in range(5):
+            lanes = slice(128 * b, 128 * (b + 1))
+            acc = rsend[CHUNKS - 1, rows, lanes].astype(f32)
+            for t in range(CHUNKS - 1):
+                acc = acc + rrecv[t, rows, lanes].astype(f32)
+            total[b] = acc
+        for g in range(8):
+            to = block * 8 + g
             for b in range(5):
-                rows = total[pl.ds(pl.multiple_of(q * 40, 8), 40), 128 * b : 128 * (b + 1)]
-                packed[b * 10 : b * 10 + 10, :] = rows[10 * i : 10 * i + 10]
-            fsend[to] = packed[...].astype(bf16)
+                packed[g, b * 10 : b * 10 + 10, :] = total[b, 10 * g : 10 * g + 10, :]
+            fsend[to] = packed[g].astype(bf16)
 
             @pl.when(is_own(to))
             def _():
@@ -403,7 +401,8 @@
 
         return 0
 
-    lax.fori_loop(0, 8, pack, 0)
+    pl.semaphore_wait(ready, RING - 1)
+    lax.fori_loop(0, 4, pack, 0)
 
     def sent(t, _):
         for u in range(3):
@@ -415,23 +414,21 @@
     for t in range(CHUNKS - 1):
         y_copy(t).wait_send()
 
-    for coef in range(2):
-        for h in range(2):
-            for at in range(RING):
-                i = (coef * 2 + h) * RING + at
-                pltpu.make_async_copy(fsend.at[0], frecv.at[i], fr_sem.at[i]).wait()
-                packed[...] = frecv[i].astype(f32)
-                for b in range(5):
-                    piece = packed[b * 10 : b * 10 + 10, :]
-                    base = coef * N + 8 * h + at
-                    if b < 4:
-                        final[b // 2, pl.ds(base + 16 * (b % 2), 10, stride=32), :] = piece
-                    else:
-                        final[2, pl.ds(base, 10, stride=32), :] = piece
-                        final[2, pl.ds(base + 16, 10, stride=32), :] = pltpu.roll(piece, 64, 1)
-    out[:, 0:128] = final[0]
-    out[:, 128:256] = final[1]
-    out[:, 256:320] = final[2][:, :64]
+    for source in range(4):
+        for at in range(RING):
+            i = source * RING + at
+            pltpu.make_async_copy(fsend.at[0], frecv.at[i], fr_sem.at[i]).wait()
+            final[source, PACKED * at : PACKED * (at + 1), :] = frecv[i].astype(f32)
+        for z in range(10):
+            for b in range(5):
+                rows = final[source, pl.ds(b * 10 + z, RING, stride=PACKED), :]
+                base = (source // 2) * N + 32 * z + 8 * (source % 2)
+                if b < 4:
+                    base += 16 * (b % 2)
+                    out[base : base + 8, 128 * (b // 2) : 128 * (b // 2 + 1)] = rows
+                else:
+                    out[base : base + 8, 256:320] = rows[:, :64]
+                    out[base + 16 : base + 24, 256:320] = pltpu.roll(rows, 64, 1)[:, :64]
 
     def left(to, _):
         @pl.when(jnp.logical_not(is_own(to)))
@@ -473,10 +470,10 @@
             vmem((2, 8, 128), f32),
             vmem((5, 640, 128), f32),
             vmem((2 * N, LANES), bf16),
-            vmem((N, LANES), f32),
-            vmem((PACKED, 128), f32),
-            vmem((3, 640, 128), f32),
-            dma((5,)), dma((7,)), dma((CHUNKS, 3)), dma((CHUNKS, 3)), dma, dma,
+            vmem((5, BLOCK, 128), f32),
+            vmem((8, PACKED, 128), f32),
+            vmem((4, RING * PACKED, 128), f32),
+            pltpu.SemaphoreType.REGULAR, dma((5,)), dma((7,)), dma((CHUNKS, 3)), dma((CHUNKS, 3)), dma, dma,
             dma((CHUNKS, 3, 7)), dma((CHUNKS, 3, 7)),
             dma((CHUNKS, 3, RING - 1)), dma((CHUNKS, 3, RING - 1)),
             dma((CHUNKS - 1,)), dma((CHUNKS - 1,)),

time: 118 us -> 116 us (0.983)
  Pallas kernels: 114 us -> 112 us
    pallas_call x1, Pallas kernels: 114 us -> 112 us  [body(): pl.pallas_call(kernel, name='shears', out_shape=jax.ShapeDtypeStruct((640...]
where the time goes in v5:
time: 116 us
  Pallas kernels  112 us (97%)
  local copies, waits for them, and re-layouts  2.22 us (2%)
  between operations  1.3 us (1%)
    pallas_call x1, Pallas kernels, body(): pl.pallas_call(kernel, name='shears', out_shape=jax.ShapeDtypeStruct((640...  112 us

profile of v5, /device:TPU:15, one launch (start us, length us, event | category | flops | bytes accessed | tf_op | source)
XLA Modules:
  0.0 115.6 jit_solution(12628004195588218435)
XLA Ops:
  1.3 112.1 %shears.1 = f32[640,320]{1,0:T(8,128)} custom-call(s32[1]{0:T(128)S(6)} %copy.11.rot_hbm, s32[1]{0:T(128)S(6)} %copy.12.counts_hbm, f32[2,32]{1,0:T(2,128)} %constant.17.clone.shifts, bf16[2,10,640,128]{3,2,1,0:T(8,128)(2,1)} %bitcast.5, bf16[640,768]{1,0:T(8,128)(2,1)} %constant.12.clone.fwd_hbm, bf16[768,640]{1,0:T(8,128)(2,1)} %constant.13.clone.inv_hbm, ...), custom_call_target="tpu_custom_call" | custom-call | flops 12999999488 | bytes 8000000 | tf_op jit(solution)/shard_map/shears/pallas_call | solution.py:450
  113.4 2.2 %copy.13 = f32[2,10,2,320,16]{3,4,2,1,0:T(8,128)} copy(f32[2,10,2,320,16]{3,4,2,1,0:T(8,128)} %bitcast.4) | data formatting | bytes 1638400

commit v6 on v5

--- a/solution.py
+++ b/solution.py
@@ -308,15 +308,19 @@
                 second[s * N : (s + 1) * N, 128 * b : 128 * (b + 1)] = (
                     both[:N, 128 * i : 128 * (i + 1)] - far[i]).astype(bf16)
 
-    def shear_x(t):
-        spectrum = jnp.dot(second[...], fwd3[...], preferred_element_type=f32)
+    def shear_x(t, half):
+        here = pl.ds(pl.multiple_of(160 * half, 16), 160)
+        there = pl.ds(pl.multiple_of(N + 160 * half, 16), 160)
+        left = jnp.concatenate([second[here, :], second[there, :]], axis=0)
+        spectrum = jnp.dot(left, fwd3[...], preferred_element_type=f32)
         re, im = spectrum[:, :PAD], spectrum[:, PAD:]
-        cosine, sine = cos_x[...], sin_x[...]
+        cosine = jnp.concatenate([cos_x[here, :], cos_x[there, :]], axis=0)
+        sine = jnp.concatenate([sin_x[here, :], sin_x[there, :]], axis=0)
         ramped = jnp.concatenate([re * cosine + im * sine, im * cosine - re * sine], axis=1).astype(bf16)
         moved = jnp.dot(ramped, inv[...], preferred_element_type=f32)
         w0 = jnp.concatenate([params[0, 2:3, :]] * 5, axis=1)
         w1 = jnp.concatenate([params[1, 2:3, :]] * 5, axis=1)
-        rsend[t] = (moved[:N] * w0 + moved[N:] * w1).astype(bf16)
+        rsend[t, here, :] = (moved[:160] * w0 + moved[160:] * w1).astype(bf16)
 
     def step(t, _):
         @pl.when(t < CHUNKS)
@@ -350,10 +354,11 @@
             for u in UNITS:
                 arrive(z_copies(t - 1, u))
                 shear_z(t - 1, u)
-            shear_x(t - 1)
 
             @pl.when(t < CHUNKS)
             def _():
+                shear_x(t - 1, 0)
+                shear_x(t - 1, 1)
                 y_copy(t - 1).start()
 
         return 0
@@ -377,7 +382,7 @@
         return jnp.logical_and(to == slab, target == state)
 
     def pack(i, _):
-        block = lax.rem(zhi + 2 + i, 4)
+        block = 2 * lax.rem(zhi // 2 + 1 + i // 2, 2) + lax.rem(zhi + i, 2)
         rows = pl.ds(pl.multiple_of(block * BLOCK, 16), BLOCK)
         for b in range(5):
             lanes = slice(128 * b, 128 * (b + 1))
@@ -402,7 +407,14 @@
         return 0
 
     pl.semaphore_wait(ready, RING - 1)
-    lax.fori_loop(0, 4, pack, 0)
+
+
+    def finish(i, _):
+        shear_x(CHUNKS - 1, lax.rem(zhi // 2 + 1 + i, 2))
+        lax.fori_loop(2 * i, 2 * i + 2, pack, 0)
+        return 0
+
+    lax.fori_loop(0, 2, finish, 0)
 
     def sent(t, _):
         for u in range(3):
@@ -413,6 +425,15 @@
     lax.fori_loop(0, CHUNKS, sent, 0)
     for t in range(CHUNKS - 1):
         y_copy(t).wait_send()
+
+    def left(to, _):
+        @pl.when(jnp.logical_not(is_own(to)))
+        def _():
+            f_copy(to).wait_send()
+
+        return 0
+
+    lax.fori_loop(0, 32, left, 0)
 
     for source in range(4):
         for at in range(RING):
@@ -429,15 +450,6 @@
                 else:
                     out[base : base + 8, 256:320] = rows[:, :64]
                     out[base + 16 : base + 24, 256:320] = pltpu.roll(rows, 64, 1)[:, :64]
-
-    def left(to, _):
-        @pl.when(jnp.logical_not(is_own(to)))
-        def _():
-            f_copy(to).wait_send()
-
-        return 0
-
-    lax.fori_loop(0, 32, left, 0)
 
 
 def body(state_images, rot_index, counts):

time: 116 us -> 115 us (level)
  no operation moved by 1% of the time
where the time goes in v6:
time: 115 us
  Pallas kernels  111 us (97%)
  local copies, waits for them, and re-layouts  2.22 us (2%)
  between operations  1.3 us (1%)
    pallas_call x1, Pallas kernels, body(): pl.pallas_call(kernel, name='shears', out_shape=jax.ShapeDtypeStruct((640...  111 us

profile of v6, /device:TPU:15, one launch (start us, length us, event | category | flops | bytes accessed | tf_op | source)
XLA Modules:
  0.0 114.9 jit_solution(5447032168549950551)
XLA Ops:
  1.3 111.4 %shears.1 = f32[640,320]{1,0:T(8,128)} custom-call(s32[1]{0:T(128)S(6)} %copy.11.rot_hbm, s32[1]{0:T(128)S(6)} %copy.12.counts_hbm, f32[2,32]{1,0:T(2,128)} %constant.17.clone.shifts, bf16[2,10,640,128]{3,2,1,0:T(8,128)(2,1)} %bitcast.5, bf16[640,768]{1,0:T(8,128)(2,1)} %constant.12.clone.fwd_hbm, bf16[768,640]{1,0:T(8,128)(2,1)} %constant.13.clone.inv_hbm, ...), custom_call_target="tpu_custom_call" | custom-call | flops 12999999488 | bytes 8000000 | tf_op jit(solution)/shard_map/shears/pallas_call | solution.py:462
  112.7 2.2 %copy.13 = f32[2,10,2,320,16]{3,4,2,1,0:T(8,128)} copy(f32[2,10,2,320,16]{3,4,2,1,0:T(8,128)} %bitcast.4) | data formatting | bytes 1638400
